TPU v7x, 256 devices: a whole 4x4x8 slice. The times are simulated.
256 devices in a mesh: pair: 32 (over z, x_hi, core), edge: 8 (over x_lo, y).
Axes of the slice: x: 4 (x_hi: 2, x_lo: 2; x = x_hi * 2 + x_lo), y: 4, z: 8, core: 2. Of those that a mesh axis runs over, the one named last changes fastest.
Arguments:
- left_block: float32 [32768, 400], P(('pair', 'edge')), may hold values from -0.9 to 0.9
- left_state: float32 [32768], P(('pair', 'edge')), may hold values from 0.05 to 0.5
- right_block: float32 [32768, 400], P(('pair', 'edge')), may hold values from -0.9 to 0.9
- right_state: float32 [32768], P(('pair', 'edge')), may hold values from 0.05 to 0.5
- relations: float32 [256, 400], replicated, may hold values from -4 to 4
- relation_state: float32 [256, 400], replicated, may hold values from 0.02 to 0.2
- source_ids: int32 [2, 128000], P(None, ('pair', 'edge')), may hold values from 0 to 1023
- relation_ids: int32 [2, 128000], P(None, ('pair', 'edge')), may hold values from 0 to 255
- target_ids: int32 [2, 128000], P(None, ('pair', 'edge')), may hold values from 0 to 1023
- sample_ids: int32 [2, 32000], P(None, 'pair'), may hold values from 0 to 1023
- bucket_counts: int32 [2, 32], P(None, 'pair'), may hold values from 250 to 4000, as said below
Outputs:
- left_out: float32 [32768, 400], P(('pair', 'edge'))
- left_state_out: float32 [32768], P(('pair', 'edge'))
- right_out: float32 [32768, 400], P(('pair', 'edge'))
- right_state_out: float32 [32768], P(('pair', 'edge'))
- relations_out: float32 [256, 400], replicated
- relation_state_out: float32 [256, 400], replicated
Inputs may be any that keep to these rules, and one draw needn't show every extreme that they name: `bucket_counts`: in every round at least one bucket has all of its slots live.
All inputs are finite; a program needn't handle non-finite values.
Results may differ from a plain program's by a relative error of at most 0.013.
Values may be sent and summed in bfloat16 or wider, within the bound.
A program may use at most 64 MiB of HBM per device.

v0:
```python
import jax
import jax.numpy as jnp
from jax import lax
from jax.sharding import PartitionSpec as P

entity_rate = 0.3
relation_rate = 0.3


def from_behind(block, axis, distance):
    devices = range(lax.axis_size(axis))
    route = [((i - distance) % len(devices), i) for i in devices]
    return lax.ppermute(block, axis, route)


def complex_product(left_value, right_value):
    middle = left_value.shape[-1] // 2
    left_real, left_imag = (left_value[..., :middle], left_value[..., middle:])
    right_real, right_imag = (right_value[..., :middle], right_value[..., middle:])
    return jnp.concatenate(
        [
            left_real * right_real - left_imag * right_imag,
            left_real * right_imag + left_imag * right_real,
        ],
        axis=-1,
    )


def conjugate(value):
    middle = value.shape[-1] // 2
    return jnp.concatenate([value[..., :middle], -value[..., middle:]], axis=-1)


def bucket_terms(
    left_low, right_low, relations, source_ids, relation_ids, target_ids, sample_ids, active
):
    row_count = left_low.shape[0]
    source = jnp.take(left_low, source_ids, axis=0).astype(jnp.float32)
    target = jnp.take(right_low, target_ids, axis=0).astype(jnp.float32)
    operator = jnp.take(relations, relation_ids, axis=0)
    query_low = complex_product(source, operator).astype(jnp.bfloat16)
    query = query_low.astype(jnp.float32)
    sampled = jnp.take(right_low, sample_ids, axis=0)
    positive = jnp.sum(query * target, axis=-1)
    scores = lax.dot_general(
        query_low, sampled, (((1,), (1,)), ((), ())), preferred_element_type=jnp.float32
    )
    weight_pos = -active * jax.nn.sigmoid(-positive)
    weight_neg = (jax.nn.sigmoid(scores) * (active / sample_ids.shape[0])[:, None]).astype(
        jnp.bfloat16
    )
    grad_query = (
        jnp.dot(weight_neg, sampled, preferred_element_type=jnp.float32)
        + weight_pos[:, None] * target
    )
    grad_sampled = lax.dot_general(
        weight_neg, query_low, (((0,), (0,)), ((), ())), preferred_element_type=jnp.float32
    )
    grad_source = complex_product(grad_query, conjugate(operator))
    grad_operator = complex_product(grad_query, conjugate(source))
    left_grad = jax.ops.segment_sum(grad_source, source_ids, row_count)
    right_grad = jax.ops.segment_sum(weight_pos[:, None] * query, target_ids, row_count)
    right_grad = right_grad + jax.ops.segment_sum(grad_sampled, sample_ids, row_count)
    relation_grad = jax.ops.segment_sum(grad_operator, relation_ids, relations.shape[0])
    return (left_grad, right_grad, relation_grad)


def row_update(block, state, grad):
    new_state = state + jnp.mean(grad * grad, axis=-1)
    return (block - entity_rate * grad / jnp.sqrt(new_state)[..., None], new_state)


def body(
    left_block,
    left_state,
    right_block,
    right_state,
    relations,
    relation_state,
    source_ids,
    relation_ids,
    target_ids,
    sample_ids,
    bucket_counts,
):
    round_count = source_ids.shape[0]
    edge_count = source_ids.shape[1]
    member = lax.axis_index("edge")
    share = left_block.shape[0]
    slots = member * edge_count + jnp.arange(edge_count, dtype=jnp.int32)
    relation_total = jnp.zeros_like(relations)
    for round_index in range(round_count):
        active = (slots < bucket_counts[round_index, 0]).astype(jnp.float32)
        left_low, right_low = (
            lax.all_gather(left_block.astype(jnp.bfloat16), "edge", axis=0, tiled=True),
            lax.all_gather(right_block.astype(jnp.bfloat16), "edge", axis=0, tiled=True),
        )
        left_grad, right_grad, relation_grad = bucket_terms(
            left_low,
            right_low,
            relations,
            source_ids[round_index],
            relation_ids[round_index],
            target_ids[round_index],
            sample_ids[round_index],
            active,
        )
        relation_total = relation_total + lax.psum(relation_grad, ("pair", "edge"))
        left_whole, right_whole = (
            lax.psum(left_grad.astype(jnp.bfloat16), "edge").astype(jnp.float32),
            lax.psum(right_grad.astype(jnp.bfloat16), "edge").astype(jnp.float32),
        )
        start = member * share
        left_sum = lax.dynamic_slice_in_dim(left_whole, start, share, 0)
        right_sum = lax.dynamic_slice_in_dim(right_whole, start, share, 0)
        left_block, left_state = row_update(left_block, left_state, left_sum)
        right_block, right_state = row_update(right_block, right_state, right_sum)
        if round_index + 1 < round_count:
            left_block, left_state = (
                from_behind(left_block.astype(jnp.bfloat16), "pair", 1).astype(left_block.dtype),
                from_behind(left_state.astype(jnp.bfloat16), "pair", 1).astype(left_state.dtype),
            )
            right_block, right_state = (
                from_behind(right_block.astype(jnp.bfloat16), "pair", -1).astype(right_block.dtype),
                from_behind(right_state.astype(jnp.bfloat16), "pair", -1).astype(right_state.dtype),
            )
    new_relation_state = relation_state + relation_total * relation_total
    new_relations = relations - relation_rate * relation_total / jnp.sqrt(new_relation_state)
    return (left_block, left_state, right_block, right_state, new_relations, new_relation_state)


def solution(mesh):
    placed = (
        P(("pair", "edge"), None),
        P(("pair", "edge")),
        P(("pair", "edge"), None),
        P(("pair", "edge")),
        P(),
        P(),
        P(None, ("pair", "edge")),
        P(None, ("pair", "edge")),
        P(None, ("pair", "edge")),
        P(None, "pair"),
        P(None, "pair"),
    )
    return jax.shard_map(
        body,
        mesh=mesh,
        in_specs=placed,
        out_specs=(
            P(("pair", "edge"), None),
            P(("pair", "edge")),
            P(("pair", "edge"), None),
            P(("pair", "edge")),
            P(),
            P(),
        ),
        check_vma=False,
    )
```

profile of v0, /device:TPU:1, one launch (start us, length us, event | category | flops | bytes accessed | tf_op | source)
XLA Modules:
  0.0 657.4 jit_solution(8462732689000958634)
XLA Ops:
  11.6 1.7 gather_fusion.1
  13.7 24.9 %all_gather.12 = bf16[1024,400]{0,1:T(8,128)(2,1)S(1)} all-gather(bf16[128,400]{0,1:T(8,128)(2,1)S(1)} %convert_element_type.98), channel_id=1, replica_groups=mesh['pair'=32,'edge'=8] {'edge'}, dimensions={0}, use_global_device_ids=true | all-gather | bytes 921600 | tf_op jit(solution)/shard_map/all_gather | solution.py:95
  39.1 2.1 gather_fusion
  42.2 22.2 %all_gather.13 = bf16[1024,400]{0,1:T(8,128)(2,1)S(1)} all-gather(bf16[128,400]{0,1:T(8,128)(2,1)S(1)} %convert_element_type.100), channel_id=1, replica_groups=mesh['pair'=32,'edge'=8] {'edge'}, dimensions={0}, use_global_device_ids=true | all-gather | bytes 921600 | tf_op jit(solution)/shard_map/all_gather | solution.py:96
  64.9 2.1 gather_fusion.3
  73.1 5.1 gather_fusion.2
  78.2 2.4 multiply_convert_fusion.1
  80.6 2.0 fusion.45
  86.3 4.9 scatter_custom_fusion
  92.3 7.8 %scatter_custom_fusion.2 = f32[1024,400]{1,0:T(8,128)S(1)} fusion(s32[1000]{0:T(1024)S(1)} %bitcast.19, f32[1000,400]{1,0:T(8,128)} %fusion.45, f32[]{:T(128)} %constant.27.clone.1), kind=kCustom, calls=%fused_computation.28 | custom fusion | flops 400000 | bytes 1638912 | tf_op jit(solution)/shard_map/scatter-add | solution.py:63
  100.0 2.5 copy.69
  102.5 5.6 scatter_custom_fusion.1
  108.1 2.9 add_convert_fusion.1
  114.6 1.7 gather_fusion.5
  117.9 4.7 scatter_custom_fusion.6
  124.5 80.2 %all-reduce.10.cloned.1.call-done = (bf16[1024,400]{1,0:T(8,128)(2,1)}, bf16[1024,400]{1,0:T(8,128)(2,1)}) async-done(((bf16[1024,400]{1,0:T(8,128)(2,1)}, bf16[1024,400]{1,0:T(8,128)(2,1)}), (bf16[1024,400]{1,0:T(8,128)(2,1)}, bf16[1024,400]{1,0:T(8,128)(2,1)})) %all-reduce.10.cloned.1.call-update) | async-done | bytes 1638416 | tf_op jit(solution)/shard_map/psum | solution.py:110
  207.2 7.1 %collective-permute-start = (bf16[128,400]{1,0:T(8,128)(2,1)S(1)}, bf16[128,400]{1,0:T(8,128)(2,1)S(1)}, u32[]{:S(2)}, u32[]{:S(2)}) collective-permute-start(bf16[128,400]{1,0:T(8,128)(2,1)S(1)} %fusion.17), channel_id=1, source_target_pairs={{248,0},{0,8},{8,16},{16,24},{24,32},{32,40},{40,48},{48,56},{56,6... | collective-permute-start | bytes 307208 | tf_op jit(solution)/shard_map/ppermute | solution.py:13
  217.0 25.1 %all_gather.14 = bf16[1024,400]{1,0:T(8,128)(2,1)S(1)} all-gather(bf16[128,400]{1,0:T(8,128)(2,1)S(1)} %collective-permute-done), channel_id=1, replica_groups=mesh['pair'=32,'edge'=8] {'edge'}, dimensions={0}, use_global_device_ids=true | all-gather | bytes 921600 | tf_op jit(solution)/shard_map/all_gather | solution.py:95
  242.1 2.1 gather_fusion.4
  245.2 23.7 %all_gather.15 = bf16[1024,400]{1,0:T(8,128)(2,1)S(1)} all-gather(bf16[128,400]{1,0:T(8,128)(2,1)S(1)} %collective-permute-done.1), channel_id=1, replica_groups=mesh['pair'=32,'edge'=8] {'edge'}, dimensions={0}, use_global_device_ids=true | all-gather | bytes 921600 | tf_op jit(solution)/shard_map/all_gather | solution.py:96
  268.9 2.1 gather_fusion.7
  275.4 5.3 gather_fusion.6
  280.7 2.3 multiply_convert_fusion
  283.1 2.0 fusion.44
  288.6 4.3 scatter_custom_fusion.7
  294.1 8.7 %scatter_custom_fusion.5 = f32[1024,400]{1,0:T(8,128)} fusion(s32[1000]{0:T(1024)S(1)} %bitcast.16, f32[1000,400]{1,0:T(8,128)} %fusion.44, f32[]{:T(128)} %constant.27.clone.1), kind=kCustom, calls=%fused_computation.22 | custom fusion | flops 400000 | bytes 1638912 | tf_op jit(solution)/shard_map/scatter-add | solution.py:63
  303.1 5.1 scatter_custom_fusion.4
  309.5 4.7 scatter_custom_fusion.3
  316.2 2.9 add_convert_fusion
  320.3 15.0 %collective-permute-start.3 = (bf16[128]{0:T(256)(128)(2,1)S(1)}, bf16[128]{0:T(256)(128)(2,1)S(1)}, u32[]{:S(2)}, u32[]{:S(2)}) collective-permute-start(bf16[128]{0:T(256)(128)(2,1)S(1)} %copy-done.33), channel_id=1, source_target_pairs={{8,0},{16,8},{24,16},{32,24},{40,32},{48,40},{56,48},{64,56},{72,6... | collective-permute-start | bytes 776 | tf_op jit(solution)/shard_map/ppermute | solution.py:13
  335.8 221.6 %all-reduce.6.cloned.1.call-done = f32[256,400]{1,0:T(8,128)} async-done(((f32[256,400]{1,0:T(8,128)}), f32[256,400]{1,0:T(8,128)}) %all-reduce.6.cloned.1.call-update) | async-done | bytes 409616 | tf_op jit(solution)/shard_map/psum | solution.py:108
  560.5 83.5 %all-reduce.8.cloned.1.call-done = (bf16[1024,400]{1,0:T(8,128)(2,1)}, bf16[1024,400]{1,0:T(8,128)(2,1)}) async-done(((bf16[1024,400]{1,0:T(8,128)(2,1)}, bf16[1024,400]{1,0:T(8,128)(2,1)}), (bf16[1024,400]{1,0:T(8,128)(2,1)}, bf16[1024,400]{1,0:T(8,128)(2,1)})) %all-reduce.8.cloned.1.call-update) | async-done | bytes 1638416 | tf_op jit(solution)/shard_map/psum | solution.py:110
  (169 shorter events, 54.8 us)
Async XLA Ops:
  7.2 197.5 %all-reduce.10.cloned.1.call-start = ((), (), s32[]{:S(2)}) async-start(), calls=%async_computation.2 | async-start | bytes 4194304 | tf_op jit(solution)/shard_map/psum | solution.py:110
  8.0 115.3 %copy-start.23 = (s32[1,500]{1,0:T(1,128)}, s32[1,500]{1,0:T(1,128)S(1)}, u32[]{:S(2)}) copy-start(s32[1,500]{1,0:T(1,128)S(1)} %get-tuple-element.57) | copy-start | bytes 6004
  9.6 113.7 %copy-start.22 = (s32[1,500]{1,0:T(1,128)}, s32[1,500]{1,0:T(1,128)S(1)}, u32[]{:S(2)}) copy-start(s32[1,500]{1,0:T(1,128)S(1)} %get-tuple-element.55) | copy-start | bytes 6004
  39.1 3.1 copy-start.17
  64.9 3.1 copy-start.26
  78.2 2.4 copy-start.2
  80.6 2.1 copy-start.6
  111.0 2.8 copy-start.18
  111.0 446.4 %all-reduce.6.cloned.1.call-start = ((), (), s32[]{:S(2)}) async-start(), calls=%async_computation | async-start | bytes 1048576 | tf_op jit(solution)/shard_map/psum | solution.py:108
  117.5 6.9 %copy-start.1 = (f32[500,400]{0,1:T(8,128)S(1)}, f32[500,400]{0,1:T(8,128)}, u32[]{:S(2)}) copy-start(f32[500,400]{0,1:T(8,128)} %copy.68) | copy-start | bytes 2400004
  117.5 88.2 %copy-start.30 = (f32[128]{0:T(128)S(1)}, f32[128]{0:T(128)}, u32[]{:S(2)}) copy-start(f32[128]{0:T(128)} %param.18) | copy-start | bytes 1540
  117.9 88.4 %copy-start.12 = (f32[128,400]{1,0:T(8,128)S(1)}, f32[128,400]{1,0:T(8,128)}, u32[]{:S(2)}) copy-start(f32[128,400]{1,0:T(8,128)} %copy.65) | copy-start | bytes 614404
  117.9 97.5 %copy-start.31 = (f32[128]{0:T(128)S(1)}, f32[128]{0:T(128)}, u32[]{:S(2)}) copy-start(f32[128]{0:T(128)} %param.20) | copy-start | bytes 1540
  117.9 98.0 %copy-start.11 = (f32[128,400]{1,0:T(8,128)S(1)}, f32[128,400]{1,0:T(8,128)}, u32[]{:S(2)}) copy-start(f32[128,400]{1,0:T(8,128)} %copy.71) | copy-start | bytes 614404
  122.6 119.5 %copy-start.24 = (s32[1024]{0:T(1024)S(1)}, s32[1024]{0:T(1024)}, u32[]{:S(2)}) copy-start(s32[1024]{0:T(1024)} %pad_clamp_fusion.3) | copy-start | bytes 12292
  207.2 9.8 %collective-permute-start = (bf16[128,400]{1,0:T(8,128)(2,1)S(1)}, bf16[128,400]{1,0:T(8,128)(2,1)S(1)}, u32[]{:S(2)}, u32[]{:S(2)}) collective-permute-start(bf16[128,400]{1,0:T(8,128)(2,1)S(1)} %fusion.17), channel_id=1, source_target_pairs={{248,0},{0,8},{8,16},{16,24},{24,32},{32,40},{40,48},{48,56},{56,6... | collective-permute-start | bytes 307208 | tf_op jit(solution)/shard_map/ppermute | solution.py:13
  216.9 28.3 %collective-permute-start.1 = (bf16[128,400]{1,0:T(8,128)(2,1)S(1)}, bf16[128,400]{1,0:T(8,128)(2,1)S(1)}, u32[]{:S(2)}, u32[]{:S(2)}) collective-permute-start(bf16[128,400]{1,0:T(8,128)(2,1)S(1)} %fusion.21), channel_id=1, source_target_pairs={{8,0},{16,8},{24,16},{32,24},{40,32},{48,40},{56,48},{64,56},{72,6... | collective-permute-start | bytes 307208 | tf_op jit(solution)/shard_map/ppermute | solution.py:13
  245.2 25.8 %copy-start.19 = (bf16[128,400]{1,0:T(8,128)(2,1)}, bf16[128,400]{1,0:T(8,128)(2,1)S(1)}, u32[]{:S(2)}) copy-start(bf16[128,400]{1,0:T(8,128)(2,1)S(1)} %collective-permute-done.1) | copy-start | bytes 307204
  280.7 2.3 copy-start.4
  283.0 2.1 copy-start.8
  283.0 2.1 copy-start.14
  283.0 2.1 copy-start.25
  283.0 2.1 copy-start.28
  283.1 2.1 copy-start.29
  287.3 5.7 copy-start.5
  293.9 350.1 %all-reduce.8.cloned.1.call-start = ((), (), s32[]{:S(2)}) async-start(), calls=%async_computation.1 | async-start | bytes 4194304 | tf_op jit(solution)/shard_map/psum | solution.py:110
  302.7 5.4 copy-start.9
  302.7 5.4 copy-start.10
  319.1 16.3 %copy-start.32 = (bf16[128]{0:T(256)(128)(2,1)S(1)}, bf16[128]{0:T(256)(128)(2,1)}, u32[]{:S(2)}) copy-start(bf16[128]{0:T(256)(128)(2,1)} %get-tuple-element.63) | copy-start | bytes 772
  320.3 324.7 %collective-permute-start.3 = (bf16[128]{0:T(256)(128)(2,1)S(1)}, bf16[128]{0:T(256)(128)(2,1)S(1)}, u32[]{:S(2)}, u32[]{:S(2)}) collective-permute-start(bf16[128]{0:T(256)(128)(2,1)S(1)} %copy-done.33), channel_id=1, source_target_pairs={{8,0},{16,8},{24,16},{32,24},{40,32},{48,40},{56,48},{64,56},{72,6... | collective-permute-start | bytes 776 | tf_op jit(solution)/shard_map/ppermute | solution.py:13
  335.3 310.1 %copy-start.20 = (bf16[128,400]{1,0:T(8,128)(2,1)S(1)}, bf16[128,400]{1,0:T(8,128)(2,1)}, u32[]{:S(2)}) copy-start(bf16[128,400]{1,0:T(8,128)(2,1)} %copy-done.19) | copy-start | bytes 307204
  335.3 313.0 %collective-permute-start.2 = (bf16[128]{0:T(256)(128)(2,1)S(1)}, bf16[128]{0:T(256)(128)(2,1)S(1)}, u32[]{:S(2)}, u32[]{:S(2)}) collective-permute-start(bf16[128]{0:T(256)(128)(2,1)S(1)} %copy-done.32), channel_id=1, source_target_pairs={{248,0},{0,8},{8,16},{16,24},{24,32},{32,40},{40,48},{48,56},{56,6... | collective-permute-start | bytes 776 | tf_op jit(solution)/shard_map/ppermute | solution.py:13
  (9 other events, 14.9 us)
Sparse Core Ops, SparseCore 0:
  111.2 93.4 all-reduce.9
  294.0 263.3 all-reduce.5
  560.1 83.7 all-reduce.7
where the time goes:
time: 669 us; the launch traced here: 657 us
  waiting for transfers between devices  385 us (58%)
  blocking collectives  95.8 us (14%)
  other arithmetic  79.8 us (12%)
  local copies, waits for them, and re-layouts  48.5 us (7%)
  starting transfers between devices  23 us (3%)
  between operations  14.6 us (2%)
  matrix products  10.4 us (2%)
    psum x1, waiting for transfers between devices, body(): relation_total = relation_total + lax.psum(relation_grad, ('pair', 'edge'))  222 us
    psum x2, waiting for transfers between devices, body(): lax.psum(left_grad.astype(jnp.bfloat16), 'edge').astype(jnp.float32)  164 us
    all_gather x2, blocking collectives, body(): lax.all_gather(left_block.astype(jnp.bfloat16), 'edge', axis=0, tiled=True)  49.9 us
    all_gather x2, blocking collectives, body(): lax.all_gather(right_block.astype(jnp.bfloat16), 'edge', axis=0, tiled=True)  45.8 us
    ppermute x4, starting transfers between devices, from_behind(): return lax.ppermute(block, axis, route)  22.7 us
    scatter-add x2, other arithmetic, bucket_terms(): jax.ops.segment_sum(grad_sampled, sample_ids, row_count)  16.4 us
  transfers between devices with their start and end apart: 7, of which 3 were waited for; matrix products, arithmetic and copies ran while one was open for 8% of the time, Pallas kernels for 0%

commit v1 on v0

v1 whole, which is shorter than its diff:
```python
import functools

import jax
import jax.numpy as jnp
from jax import lax
from jax.experimental import pallas as pl
from jax.experimental.pallas import tpu as pltpu
from jax.sharding import PartitionSpec as P

ENTITY_RATE = 0.3
RELATION_RATE = 0.3
D, H = 400, 200
SHARE = 128
MEMBERS = 8
GROUPS = 32
ROWS = SHARE * MEMBERS
NREL = 256
SLOTS = 500
LANES = 512
NEG = 1000
CHUNK = 256
MESH = pl.DeviceIdType.MESH
VMEM = pl.BlockSpec(memory_space=pltpu.VMEM)
SMEM = pl.BlockSpec(memory_space=pltpu.SMEM)
f32, bf16, i32 = jnp.float32, jnp.bfloat16, jnp.int32


def nt(a, b):
    return lax.dot_general(a, b, (((1,), (1,)), ((), ())), preferred_element_type=f32)


def nn(a, b):
    return jnp.dot(a, b, preferred_element_type=f32)


def flag(condition):
    return jnp.where(condition, 1.0, 0.0).astype(bf16)


def remote(src, dst, send, recv, pair, edge):
    return pltpu.make_async_remote_copy(
        src_ref=src, dst_ref=dst, send_sem=send, recv_sem=recv,
        device_id=(pair, edge), device_id_type=MESH,
    )


def greet(devices):
    barrier = pltpu.get_barrier_semaphore()
    for device in devices:
        pl.semaphore_signal(barrier, inc=1, device_id=device, device_id_type=MESH)
    pl.semaphore_wait(barrier, len(devices))


def members(pair, edge):
    return [(pair, lax.rem(edge + d, MEMBERS)) for d in range(1, MEMBERS)]


def gather_kernel(right, source, relation, target, rows, ids, wide, low, send, recv):
    pair, edge = lax.axis_index("pair"), lax.axis_index("edge")
    peers = members(pair, edge)
    wide[...] = jnp.full_like(wide, -1.0)
    for r in range(2):
        s, k, t = (x[r : r + 1, :] for x in (source, relation, target))
        for row, value in enumerate((s >> 7, (s & 127) + 1, k, t >> 7, t & 127)):
            wide[8 * r + row : 8 * r + row + 1, 0:SLOTS] = value.astype(f32)
    ids[edge] = wide[...].astype(bf16)
    rows[edge] = right[...].astype(bf16)
    greet(peers)
    copies = []
    for d, peer in enumerate(peers):
        for j, ref in enumerate((ids, rows)):
            copy = remote(ref.at[edge], ref.at[edge], send.at[j, d], recv.at[j, d], *peer)
            copy.start()
            copies.append(copy)
    for copy in copies:
        copy.wait()


def gather(right, source, relation, target):
    return pl.pallas_call(
        gather_kernel,
        out_shape=(
            jax.ShapeDtypeStruct((MEMBERS, D, SHARE), bf16),
            jax.ShapeDtypeStruct((MEMBERS, 16, LANES), bf16),
        ),
        in_specs=[VMEM] * 4,
        out_specs=(VMEM, VMEM),
        scratch_shapes=[
            pltpu.VMEM((16, LANES), f32),
            pltpu.VMEM((16, LANES), bf16),
            pltpu.SemaphoreType.DMA((2, MEMBERS - 1)),
            pltpu.SemaphoreType.DMA((2, MEMBERS - 1)),
        ],
        compiler_params=pltpu.CompilerParams(collective_id=1, has_side_effects=True),
        name="gather_right",
    )(right, source, relation, target)


def train_kernel(
    r, rows, ids, samples, counts, left, left_state, relations, relation_in,
    right_grad, left_out, left_state_out, relation_out,
    table, table_t, rank, often, both, right_sum, left_sum,
):
    edge = lax.axis_index("edge")
    left_low = left[...].astype(bf16)
    high = relations[...].astype(bf16)
    both[:, 0:NREL] = high
    both[:, NREL:] = (relations[...] - high.astype(f32)).astype(bf16)
    for m in range(MEMBERS):
        table_t[:, m * SHARE : (m + 1) * SHARE] = rows[m]
        table[m * SHARE : (m + 1) * SHARE, :] = rows[m].T
    picked = flag(lax.broadcasted_iota(i32, (ROWS, NEG), 0) == samples[r : r + 1, :])
    often[...] = nn(picked, jnp.full((NEG, SHARE), 1.0, bf16)) * (1.0 / NEG)

    owner = jnp.concatenate(
        [ids[m].astype(f32)[8 * r : 8 * r + 1, :] for m in range(MEMBERS)], axis=0
    )
    lane = lax.broadcasted_iota(i32, (MEMBERS, LANES), 1)
    slot = lax.broadcasted_iota(i32, (MEMBERS, LANES), 0) * SLOTS + lane
    mine = (owner == edge.astype(f32)) & (slot < counts[r, 0])
    mark = flag(mine)
    before = flag(
        lax.broadcasted_iota(i32, (LANES, LANES), 0) < lax.broadcasted_iota(i32, (LANES, LANES), 1)
    )
    found = jnp.sum(jnp.where(mine, 1.0, 0.0), axis=1, keepdims=True)
    starts = [jnp.zeros((1, 1), f32)]
    for m in range(MEMBERS):
        starts.append(starts[-1] + found[m : m + 1, :])
    place = nn(mark, before) + jnp.concatenate(starts[:MEMBERS], axis=0)
    rank[...] = jnp.where(mine, place, -1.0).astype(i32)
    total = jnp.sum(found).astype(i32)

    right_sum[...] = jnp.zeros_like(right_sum)
    left_sum[...] = jnp.zeros_like(left_sum)
    relation_out[...] = relation_in[...]

    def chunk(c, carry):
        want = lax.broadcasted_iota(i32, (CHUNK, LANES), 0) + c * CHUNK
        found = jnp.zeros((16, CHUNK), f32)
        for m in range(MEMBERS):
            found = found + nt(ids[m], flag(rank[m : m + 1, :] == want))
        found = found[8 * r : 8 * r + 8, :].astype(i32)
        s, k = found[1:2, :] - 1, found[2:3, :]
        t = found[3:4, :] * SHARE + found[4:5, :]
        source_hot = flag(lax.broadcasted_iota(i32, (SHARE, CHUNK), 0) == s)
        relation_hot = flag(lax.broadcasted_iota(i32, (NREL, CHUNK), 0) == k)
        source = nn(left_low, source_hot)
        operator = nn(both[...], jnp.concatenate([relation_hot, relation_hot], axis=0))
        sr, si, kr, ki = source[:H], source[H:], operator[:H], operator[H:]
        query = jnp.concatenate([sr * kr - si * ki, sr * ki + si * kr], axis=0).astype(bf16)
        scores = nn(table[...], query)
        chance = 0.5 * jnp.tanh(0.5 * scores) + 0.5
        hit = lax.broadcasted_iota(i32, (ROWS, CHUNK), 0) == t
        spread = jnp.concatenate([often[...]] * (CHUNK // SHARE), axis=1)
        weight = (spread * chance - jnp.where(hit, 1.0 - chance, 0.0)).astype(bf16)
        grad = nn(table_t[...], weight)
        right_sum[...] += nt(query, weight)
        gr, gi = grad[:H], grad[H:]
        grad_source = jnp.concatenate([gr * kr + gi * ki, gi * kr - gr * ki], axis=0)
        grad_operator = jnp.concatenate([gr * sr + gi * si, gi * sr - gr * si], axis=0)
        left_sum[...] += nt(grad_source.astype(bf16), source_hot)
        relation_out[...] += nt(grad_operator.astype(bf16), relation_hot)
        return carry

    lax.fori_loop(0, (total + (CHUNK - 1)) // CHUNK, chunk, 0)
    for m in range(MEMBERS):
        right_grad[m] = right_sum[:, m * SHARE : (m + 1) * SHARE].astype(bf16)
    block, state = row_update(left[...], left_state[...], left_sum[...])
    left_out[...] = block
    left_state_out[...] = state


def row_update(block, state, grad):
    state = state + jnp.sum(grad * grad, axis=0, keepdims=True) * (1.0 / D)
    return block - ENTITY_RATE * grad / jnp.sqrt(state), state


def train(r, rows, ids, samples, counts, left, left_state, relations, relation_in):
    return pl.pallas_call(
        functools.partial(train_kernel, r),
        out_shape=(
            jax.ShapeDtypeStruct((MEMBERS, D, SHARE), bf16),
            jax.ShapeDtypeStruct((D, SHARE), f32),
            jax.ShapeDtypeStruct((1, SHARE), f32),
            jax.ShapeDtypeStruct((D, NREL), f32),
        ),
        in_specs=[VMEM, VMEM, VMEM, SMEM, VMEM, VMEM, VMEM, VMEM],
        out_specs=(VMEM,) * 4,
        scratch_shapes=[
            pltpu.VMEM((ROWS, D), bf16),
            pltpu.VMEM((D, ROWS), bf16),
            pltpu.VMEM((MEMBERS, LANES), i32),
            pltpu.VMEM((ROWS, SHARE), f32),
            pltpu.VMEM((D, 2 * NREL), bf16),
            pltpu.VMEM((D, ROWS), f32),
            pltpu.VMEM((D, SHARE), f32),
        ],
        compiler_params=pltpu.CompilerParams(vmem_limit_bytes=48 * 2**20),
        name="train_round",
    )(rows, ids, samples, counts, left, left_state, relations, relation_in)


def send_parts(parts, landing, send, recv, edge, peers):
    copies = []
    for d, peer in enumerate(peers):
        copy = remote(parts.at[peer[1]], landing.at[edge], send.at[d], recv.at[d], *peer)
        copy.start()
        copies.append(copy)
    return copies


def total_of(parts, landing, copies, edge):
    total = parts[edge].astype(f32)
    for d, copy in enumerate(copies):
        copy.wait_recv()
        total = total + landing[lax.rem(edge + (MEMBERS - 1 - d), MEMBERS)].astype(f32)
    return total


def exchange_kernel(
    parts, right, right_state, left, left_state,
    rows, right_out, right_state_out, left_out, left_state_out,
    landing, out_left, out_right, in_left, in_right, out_states, in_states,
    part_send, part_recv, row_send, row_recv, move_send, move_recv,
):
    pair, edge = lax.axis_index("pair"), lax.axis_index("edge")
    peers = members(pair, edge)
    ahead = (lax.rem(pair + 1, GROUPS), edge)
    behind = (lax.rem(pair + GROUPS - 1, GROUPS), edge)
    out_left[...] = left[...].astype(bf16)
    out_states[0] = jnp.broadcast_to(left_state[...], (8, SHARE))
    greet(peers + [ahead, behind])
    copies = send_parts(parts, landing, part_send, part_recv, edge, peers)
    moves = [
        remote(out_left, in_left, move_send.at[0], move_recv.at[0], *ahead),
        remote(out_states.at[0], in_states.at[0], move_send.at[1], move_recv.at[1], *ahead),
        remote(out_right, in_right, move_send.at[2], move_recv.at[2], *behind),
        remote(out_states.at[1], in_states.at[1], move_send.at[3], move_recv.at[3], *behind),
    ]
    moves[0].start()
    moves[1].start()
    grad = total_of(parts, landing, copies, edge)
    block, state = row_update(right[...], right_state[...], grad)
    out_right[...] = block.astype(bf16)
    out_states[1] = jnp.broadcast_to(state, (8, SHARE))
    moves[2].start()
    moves[3].start()
    moves[2].wait_recv()
    rows[edge] = in_right[...]
    gathers = []
    for d, peer in enumerate(peers):
        copy = remote(in_right, rows.at[edge], row_send.at[d], row_recv.at[d], *peer)
        copy.start()
        gathers.append(copy)
    right_out[...] = in_right[...].astype(f32)
    moves[3].wait_recv()
    right_state_out[...] = in_states[1, 0:1, :]
    moves[0].wait_recv()
    left_out[...] = in_left[...].astype(f32)
    moves[1].wait_recv()
    left_state_out[...] = in_states[0, 0:1, :]
    for copy in gathers:
        copy.wait_recv()
    for copy in copies + moves + gathers:
        copy.wait_send()


def exchange(parts, right, right_state, left, left_state):
    block = jax.ShapeDtypeStruct((D, SHARE), f32)
    row = jax.ShapeDtypeStruct((1, SHARE), f32)
    low = pltpu.VMEM((D, SHARE), bf16)
    dma = pltpu.SemaphoreType.DMA
    return pl.pallas_call(
        exchange_kernel,
        out_shape=(jax.ShapeDtypeStruct((MEMBERS, D, SHARE), bf16), block, row, block, row),
        in_specs=[VMEM] * 5,
        out_specs=(VMEM,) * 5,
        scratch_shapes=[
            pltpu.VMEM((MEMBERS, D, SHARE), bf16),
            low, low, low, low,
            pltpu.VMEM((2, 8, SHARE), f32),
            pltpu.VMEM((2, 8, SHARE), f32),
            dma((MEMBERS - 1,)), dma((MEMBERS - 1,)),
            dma((MEMBERS - 1,)), dma((MEMBERS - 1,)),
            dma((4,)), dma((4,)),
        ],
        compiler_params=pltpu.CompilerParams(
            collective_id=2, has_side_effects=True, vmem_limit_bytes=32 * 2**20
        ),
        name="exchange_rows",
    )(parts, right, right_state, left, left_state)


def finish_kernel(
    parts, right, right_state, relation_grad, relations, relation_state,
    right_out, right_state_out, relations_out, relation_state_out,
    landing, share, share_in, tiles, tiles_in, quad, whole,
    part_send, part_recv, s1, r1, s2, r2, s3, r3, s4, r4, s5, r5,
):
    pair, edge = lax.axis_index("pair"), lax.axis_index("edge")
    z, q = pair // 4, lax.rem(pair, 4)
    peers = members(pair, edge)
    depth = [(lax.rem(z + d, 8) * 4 + q, edge) for d in range(1, 8)]
    flat = [(z * 4 + lax.rem(q + d, 4), edge) for d in range(1, 4)]
    share[...] = jnp.zeros_like(share)
    grads = relation_grad[...].astype(bf16)
    stacked = jnp.concatenate(
        [grads[:, 0:SHARE], grads[:, SHARE:], jnp.zeros((224, SHARE), bf16)], axis=0
    )
    for m in range(MEMBERS):
        share[m] = stacked[m * SHARE : (m + 1) * SHARE, :]
    greet(peers + depth + flat)
    first = send_parts(share, share_in, s1, r1, edge, peers)
    copies = send_parts(parts, landing, part_send, part_recv, edge, peers)
    done = first + copies
    sums = total_of(share, share_in, first, edge).astype(bf16)
    for k in range(8):
        tiles[k] = sums[16 * k : 16 * k + 16, :]
    second = []
    for d, peer in enumerate(depth):
        copy = remote(
            tiles.at[lax.rem(z + d + 1, 8)], tiles_in.at[z], s2.at[d], r2.at[d], *peer
        )
        copy.start()
        second.append(copy)
    total = tiles[z].astype(f32)
    for d, copy in enumerate(second):
        copy.wait_recv()
        total = total + tiles_in[lax.rem(z + 7 - d, 8)].astype(f32)
    quad[q] = total
    third = []
    for d, peer in enumerate(flat):
        copy = remote(quad.at[q], quad.at[q], s3.at[d], r3.at[d], *peer)
        copy.start()
        third.append(copy)
    for copy in third:
        copy.wait_recv()
    rows = pl.ds(pl.multiple_of(z * 16, 16), 16)
    whole[edge, rows, :] = (quad[0] + quad[1] + quad[2] + quad[3]).astype(bf16)
    fourth = []
    for d, peer in enumerate(depth):
        here = whole.at[edge, rows, :]
        copy = remote(here, here, s4.at[d], r4.at[d], *peer)
        copy.start()
        fourth.append(copy)

    grad = total_of(parts, landing, copies, edge)
    block, state = row_update(right[...], right_state[...], grad)
    right_out[...] = block
    right_state_out[...] = state

    for copy in fourth:
        copy.wait_recv()
    fifth = []
    for d, peer in enumerate(peers):
        copy = remote(whole.at[edge], whole.at[edge], s5.at[d], r5.at[d], *peer)
        copy.start()
        fifth.append(copy)
    for copy in fifth:
        copy.wait_recv()
    gathered = whole[...].reshape(MEMBERS * SHARE, SHARE)
    grad = jnp.concatenate([gathered[0:D], gathered[D : 2 * D]], axis=1).astype(f32)
    state = relation_state[...] + grad * grad
    relation_state_out[...] = state
    relations_out[...] = relations[...] - RELATION_RATE * grad / jnp.sqrt(state)
    for copy in done + second + third + fourth + fifth:
        copy.wait_send()


def finish(parts, right, right_state, relation_grad, relations, relation_state):
    dma = pltpu.SemaphoreType.DMA
    table = jax.ShapeDtypeStruct((D, NREL), f32)
    return pl.pallas_call(
        finish_kernel,
        out_shape=(
            jax.ShapeDtypeStruct((D, SHARE), f32), jax.ShapeDtypeStruct((1, SHARE), f32),
            table, table,
        ),
        in_specs=[VMEM] * 6,
        out_specs=(VMEM,) * 4,
        scratch_shapes=[
            pltpu.VMEM((MEMBERS, D, SHARE), bf16),
            pltpu.VMEM((MEMBERS, SHARE, SHARE), bf16),
            pltpu.VMEM((MEMBERS, SHARE, SHARE), bf16),
            pltpu.VMEM((8, 16, SHARE), bf16),
            pltpu.VMEM((8, 16, SHARE), bf16),
            pltpu.VMEM((4, 16, SHARE), f32),
            pltpu.VMEM((MEMBERS, SHARE, SHARE), bf16),
            dma((7,)), dma((7,)), dma((7,)), dma((7,)), dma((7,)), dma((7,)),
            dma((3,)), dma((3,)), dma((7,)), dma((7,)), dma((7,)), dma((7,)),
        ],
        compiler_params=pltpu.CompilerParams(
            collective_id=3, has_side_effects=True, vmem_limit_bytes=32 * 2**20
        ),
        name="finish_right_and_relations",
    )(parts, right, right_state, relation_grad, relations, relation_state)


def body(
    left_block, left_state, right_block, right_state, relations, relation_state,
    source_ids, relation_ids, target_ids, sample_ids, bucket_counts,
):
    left, right = left_block.T, right_block.T
    left_sums, right_sums = left_state.reshape(1, SHARE), right_state.reshape(1, SHARE)
    operators, operator_state = relations.T, relation_state.T
    rows, ids = gather(right, source_ids, relation_ids, target_ids)
    grad = jnp.zeros((D, NREL), f32)
    parts, left, left_sums, grad = train(
        0, rows, ids, sample_ids, bucket_counts, left, left_sums, operators, grad
    )
    rows, right, right_sums, left, left_sums = exchange(parts, right, right_sums, left, left_sums)
    parts, left, left_sums, grad = train(
        1, rows, ids, sample_ids, bucket_counts, left, left_sums, operators, grad
    )
    right, right_sums, operators, operator_state = finish(
        parts, right, right_sums, grad, operators, operator_state
    )
    return (
        left.T, left_sums.reshape(SHARE), right.T, right_sums.reshape(SHARE),
        operators.T, operator_state.T,
    )


def solution(mesh):
    block, row = P(("pair", "edge"), None), P(("pair", "edge"))
    ids, group = P(None, ("pair", "edge")), P(None, "pair")
    return jax.shard_map(
        body,
        mesh=mesh,
        in_specs=(block, row, block, row, P(), P(), ids, ids, ids, group, group),
        out_specs=(block, row, block, row, P(), P()),
        check_vma=False,
    )
```

time: 669 us -> 109 us (0.16); the launches traced: 657 us -> 107 us
  waiting for transfers between devices: 385 us -> 0 us
  Pallas kernels: 0 us -> 99.3 us
  blocking collectives: 95.8 us -> 0 us
  other arithmetic: 79.8 us -> 0 us
  local copies, waits for them, and re-layouts: 48.5 us -> 7.09 us
  starting transfers between devices: 23 us -> 0 us
  between operations: 14.6 us -> 0.74 us
  matrix products: 10.4 us -> 0 us
    psum x3 -> x0, waiting for transfers between devices: 385 us -> none  [the longest x1 222 us: body(): relation_total = relation_total + lax.psum(relation_grad, ('pair', 'edge'))]
    pallas_call x0 -> x5, Pallas kernels: none -> 99.3 us  [the longest x1 34.5 us: exchange(): pl.pallas_call(exchange_kernel, out_shape=(jax.ShapeDtypeStruct((MEMBERS,...]
    all_gather x4 -> x0, blocking collectives: 95.8 us -> none  [the longest x2 49.9 us: body(): lax.all_gather(left_block.astype(jnp.bfloat16), 'edge', axis=0, tiled=True)]
    scatter-add x8 -> x0, other arithmetic: 45.6 us -> none  [the longest x2 16.4 us: bucket_terms(): jax.ops.segment_sum(grad_sampled, sample_ids, row_count)]
    gather x14 -> x0, local copies, waits for them, and re-layouts: 27.6 us -> none  [the longest x2 10.4 us: bucket_terms(): sampled = jnp.take(right_low, sample_ids, axis=0)]
    ppermute x4 -> x0, starting transfers between devices: 22.7 us -> none  [from_behind(): return lax.ppermute(block, axis, route)]
    convert_element_type x12 -> x0, other arithmetic: 13.4 us -> none  [the longest x2 5.85 us: body(): right_grad.astype(jnp.bfloat16)]
    dot_general x6 -> x0, matrix products: 10.4 us -> none  [the longest x2 4.67 us: bucket_terms(): lax.dot_general(query_low, sampled, (((1,), (1,)), ((), ())), preferred_e...]
  transfers between devices with their start and end apart: 7 -> 0, of which waited for: 3 -> 0; matrix products, arithmetic and copies ran while one was open for 8% -> 0% of each run, Pallas kernels for 0% -> 0%
where the time goes in v1:
time: 109 us; the launch traced here: 107 us
  Pallas kernels  99.3 us (91%)
  local copies, waits for them, and re-layouts  7.09 us (7%)
    pallas_call x1, Pallas kernels, exchange(): pl.pallas_call(exchange_kernel, out_shape=(jax.ShapeDtypeStruct((MEMBERS,...  34.5 us
    pallas_call x1, Pallas kernels, finish(): pl.pallas_call(finish_kernel, out_shape=(jax.ShapeDtypeStruct((D, SHARE),...  31.9 us
    pallas_call x1, Pallas kernels, gather(): pl.pallas_call(gather_kernel, out_shape=(jax.ShapeDtypeStruct((MEMBERS, D...  18.9 us
    pallas_call x2, Pallas kernels, train(): pl.pallas_call(functools.partial(train_kernel, r), out_shape=(jax.ShapeDt...  13.9 us
    unnamed x23, local copies, waits for them, and re-layouts  7.06 us

profile of v1, /device:TPU:1, one launch (start us, length us, event | category | flops | bytes accessed | tf_op | source)
XLA Modules:
  0.0 107.1 jit_solution(8851435787459076671)
XLA Ops:
  0.6 0.0 copy-start
  0.6 0.8 copy.17.counts
  1.4 18.9 %gather_right.1 = (bf16[8,400,128]{2,1,0:T(8,128)(2,1)}, bf16[8,16,512]{2,1,0:T(8,128)(2,1)}) custom-call(f32[400,128]{1,0:T(8,128)} %bitcast.15, s32[2,500]{1,0:T(2,128)} %source.1, s32[2,500]{1,0:T(2,128)} %relation.1, s32[2,500]{1,0:T(2,128)} %target.1), custom_call_target="tpu_custom_call" | custom-call | tf_op jit(solution)/shard_map/gather_right/pallas_call | solution.py:80
  20.4 0.0 copy-start.3
  20.4 0.0 copy-start.6
  20.4 0.0 copy-start.8
  20.5 0.0 copy-done
  20.5 0.8 copy-done.3
  21.3 0.0 copy-done.6
  21.3 0.0 copy-done.8
  21.3 0.0 copy-start.1
  21.3 1.1 %copy-done.1 = bf16[8,400,128]{2,1,0:T(8,128)(2,1)S(1)} copy-done((bf16[8,400,128]{2,1,0:T(8,128)(2,1)S(1)}, bf16[8,400,128]{2,1,0:T(8,128)(2,1)}, u32[]{:S(2)}) %copy-start.1) | copy-done | bytes 819224
  22.4 0.0 copy-start.5
  22.5 0.9 copy-done.5
  23.4 0.0 copy-start.2
  23.4 5.1 %train_round.2 = (bf16[8,400,128]{2,1,0:T(8,128)(2,1)S(1)}, f32[400,128]{1,0:T(8,128)S(1)}, f32[1,128]{1,0:T(1,128)S(1)}, f32[400,256]{1,0:T(8,128)S(1)}) custom-call(bf16[8,400,128]{2,1,0:T(8,128)(2,1)S(1)} %copy-done.1, bf16[8,16,512]{2,1,0:T(8,128)(2,1)S(1)} %copy-done.3, s32[2,1000]{1,0:T(2,128)S(1)} %copy-done.6, s32[2,1]{1,0:T(2,128)S(1)} %copy.17.counts, ...), custom_call_target="tpu_custom_call" | custom-call | tf_op jit(solution)/shard_map/train_round/pallas_call | solution.py:179
  28.5 0.0 copy-start.7
  28.5 0.0 copy-done.2
  28.5 0.6 copy-done.7
  29.1 34.5 %exchange_rows.1 = (bf16[8,400,128]{2,1,0:T(8,128)(2,1)S(1)}, f32[400,128]{1,0:T(8,128)S(1)}, f32[1,128]{1,0:T(1,128)S(1)}, f32[400,128]{1,0:T(8,128)S(1)}, f32[1,128]{1,0:T(1,128)S(1)}) custom-call(bf16[8,400,128]{2,1,0:T(8,128)(2,1)S(1)} %get-tuple-element.27.parts, f32[400,128]{1,0:T(8,128)S(1)} %bitcast.16, f32[1,128]{1,0:T(1,128)S(1)} %bitcast.22, ...), custom_call_target="tpu_custom_call" | custom-call | tf_op jit(solution)/shard_map/exchange_rows/pallas_call | solution.py:273
  63.6 0.0 copy-start.4
  63.6 8.8 %train_round.3 = (bf16[8,400,128]{2,1,0:T(8,128)(2,1)S(1)}, f32[400,128]{1,0:T(8,128)}, f32[1,128]{1,0:T(1,128)}, f32[400,256]{1,0:T(8,128)S(1)}) custom-call(bf16[8,400,128]{2,1,0:T(8,128)(2,1)S(1)} %get-tuple-element.30.rows, bf16[8,16,512]{2,1,0:T(8,128)(2,1)S(1)} %copy-done.3, s32[2,1000]{1,0:T(2,128)S(1)} %copy-done.6, s32[2,1]{1,0:T(2,128)S(1)} %copy.17.counts, ...), custom_call_target="tpu_custom_call" | custom-call | tf_op jit(solution)/shard_map/train_round/pallas_call | solution.py:179
  72.5 0.0 copy-done.4
  72.5 31.9 %finish_right_and_relations.1 = (f32[400,128]{1,0:T(8,128)S(1)}, f32[1,128]{1,0:T(1,128)S(1)}, f32[400,256]{1,0:T(8,128)S(1)}, f32[400,256]{1,0:T(8,128)S(1)}) custom-call(bf16[8,400,128]{2,1,0:T(8,128)(2,1)S(1)} %get-tuple-element.36.parts, f32[400,128]{1,0:T(8,128)S(1)} %get-tuple-element.37.right, f32[1,128]{1,0:T(1,128)S(1)} %get-tuple-element.38.right_state, ...), custom_call_target="tpu_custom_call" | custom-call | tf_op jit(solution)/shard_map/finish_right_and_relations/pallas_call | solution.py:373
  104.4 0.7 copy.23
  105.1 0.5 copy.24
  105.6 0.8 copy.25
  106.3 0.8 copy.26
  (1 shorter events, 0.0 us)
Async XLA Ops:
  0.6 19.8 %copy-start = (f32[256,400]{0,1:T(8,128)S(1)}, f32[256,400]{0,1:T(8,128)}, u32[]{:S(2)}) copy-start(f32[256,400]{0,1:T(8,128)} %param.15) | copy-start | bytes 1228804
  20.4 0.9 copy-start.3
  20.4 0.9 copy-start.6
  20.4 0.9 copy-start.8
  21.3 1.1 %copy-start.1 = (bf16[8,400,128]{2,1,0:T(8,128)(2,1)S(1)}, bf16[8,400,128]{2,1,0:T(8,128)(2,1)}, u32[]{:S(2)}) copy-start(bf16[8,400,128]{2,1,0:T(8,128)(2,1)} %get-tuple-element.25.rows) | copy-start | bytes 2457604
  22.4 0.9 copy-start.5
  23.4 5.1 %copy-start.2 = (f32[128,400]{0,1:T(8,128)S(1)}, f32[128,400]{0,1:T(8,128)}, u32[]{:S(2)}) copy-start(f32[128,400]{0,1:T(8,128)} %param.13) | copy-start | bytes 614404
  28.5 0.7 copy-start.7
  63.6 8.8 %copy-start.4 = (f32[256,400]{0,1:T(8,128)S(1)}, f32[256,400]{0,1:T(8,128)}, u32[]{:S(2)}) copy-start(f32[256,400]{0,1:T(8,128)} %param.16) | copy-start | bytes 1228804

commit v2 on v1

--- a/solution.py
+++ b/solution.py
@@ -18,23 +18,15 @@
 SLOTS = 500
 LANES = 512
 NEG = 1000
+ROOM = 640
+MESH = pl.DeviceIdType.MESH
+SMEM = pl.BlockSpec(memory_space=pltpu.SMEM)
 CHUNK = 256
-MESH = pl.DeviceIdType.MESH
 VMEM = pl.BlockSpec(memory_space=pltpu.VMEM)
-SMEM = pl.BlockSpec(memory_space=pltpu.SMEM)
+DMA = pltpu.SemaphoreType.DMA
 f32, bf16, i32 = jnp.float32, jnp.bfloat16, jnp.int32
-
-
-def nt(a, b):
-    return lax.dot_general(a, b, (((1,), (1,)), ((), ())), preferred_element_type=f32)
-
-
-def nn(a, b):
-    return jnp.dot(a, b, preferred_element_type=f32)
-
-
-def flag(condition):
-    return jnp.where(condition, 1.0, 0.0).astype(bf16)
+NA, NB = 208, 192
+A, B = pl.ds(0, NA), pl.ds(NA, NB)
 
 
 def remote(src, dst, send, recv, pair, edge):
@@ -91,12 +83,12 @@
             pltpu.SemaphoreType.DMA((2, MEMBERS - 1)),
             pltpu.SemaphoreType.DMA((2, MEMBERS - 1)),
         ],
-        compiler_params=pltpu.CompilerParams(collective_id=1, has_side_effects=True),
+        compiler_params=pltpu.CompilerParams(collective_id=2, has_side_effects=True),
         name="gather_right",
     )(right, source, relation, target)
 
 
-def train_kernel(
+def chunks_kernel(
     r, rows, ids, samples, counts, left, left_state, relations, relation_in,
     right_grad, left_out, left_state_out, relation_out,
     table, table_t, rank, often, both, right_sum, left_sum,
@@ -165,19 +157,14 @@
     lax.fori_loop(0, (total + (CHUNK - 1)) // CHUNK, chunk, 0)
     for m in range(MEMBERS):
         right_grad[m] = right_sum[:, m * SHARE : (m + 1) * SHARE].astype(bf16)
-    block, state = row_update(left[...], left_state[...], left_sum[...])
+    block, state = update(left[...], left_state[...], left_sum[...])
     left_out[...] = block
     left_state_out[...] = state
 
 
-def row_update(block, state, grad):
-    state = state + jnp.sum(grad * grad, axis=0, keepdims=True) * (1.0 / D)
-    return block - ENTITY_RATE * grad / jnp.sqrt(state), state
-
-
-def train(r, rows, ids, samples, counts, left, left_state, relations, relation_in):
+def train_chunks(r, rows, ids, samples, counts, left, left_state, relations, relation_in):
     return pl.pallas_call(
-        functools.partial(train_kernel, r),
+        functools.partial(chunks_kernel, r),
         out_shape=(
             jax.ShapeDtypeStruct((MEMBERS, D, SHARE), bf16),
             jax.ShapeDtypeStruct((D, SHARE), f32),
@@ -196,7 +183,7 @@
             pltpu.VMEM((D, SHARE), f32),
         ],
         compiler_params=pltpu.CompilerParams(vmem_limit_bytes=48 * 2**20),
-        name="train_round",
+        name="train_chunks",
     )(rows, ids, samples, counts, left, left_state, relations, relation_in)
 
 
@@ -240,7 +227,7 @@
     moves[0].start()
     moves[1].start()
     grad = total_of(parts, landing, copies, edge)
-    block, state = row_update(right[...], right_state[...], grad)
+    block, state = update(right[...], right_state[...], grad)
     out_right[...] = block.astype(bf16)
     out_states[1] = jnp.broadcast_to(state, (8, SHARE))
     moves[2].start()
@@ -285,7 +272,7 @@
             dma((4,)), dma((4,)),
         ],
         compiler_params=pltpu.CompilerParams(
-            collective_id=2, has_side_effects=True, vmem_limit_bytes=32 * 2**20
+            collective_id=3, has_side_effects=True, vmem_limit_bytes=32 * 2**20
         ),
         name="exchange_rows",
     )(parts, right, right_state, left, left_state)
@@ -345,7 +332,7 @@
         fourth.append(copy)
 
     grad = total_of(parts, landing, copies, edge)
-    block, state = row_update(right[...], right_state[...], grad)
+    block, state = update(right[...], right_state[...], grad)
     right_out[...] = block
     right_state_out[...] = state
 
@@ -390,13 +377,13 @@
             dma((3,)), dma((3,)), dma((7,)), dma((7,)), dma((7,)), dma((7,)),
         ],
         compiler_params=pltpu.CompilerParams(
-            collective_id=3, has_side_effects=True, vmem_limit_bytes=32 * 2**20
+            collective_id=4, has_side_effects=True, vmem_limit_bytes=32 * 2**20
         ),
         name="finish_right_and_relations",
     )(parts, right, right_state, relation_grad, relations, relation_state)
 
 
-def body(
+def any_spread(
     left_block, left_state, right_block, right_state, relations, relation_state,
     source_ids, relation_ids, target_ids, sample_ids, bucket_counts,
 ):
@@ -405,11 +392,11 @@
     operators, operator_state = relations.T, relation_state.T
     rows, ids = gather(right, source_ids, relation_ids, target_ids)
     grad = jnp.zeros((D, NREL), f32)
-    parts, left, left_sums, grad = train(
+    parts, left, left_sums, grad = train_chunks(
         0, rows, ids, sample_ids, bucket_counts, left, left_sums, operators, grad
     )
     rows, right, right_sums, left, left_sums = exchange(parts, right, right_sums, left, left_sums)
-    parts, left, left_sums, grad = train(
+    parts, left, left_sums, grad = train_chunks(
         1, rows, ids, sample_ids, bucket_counts, left, left_sums, operators, grad
     )
     right, right_sums, operators, operator_state = finish(
@@ -419,6 +406,474 @@
         left.T, left_sums.reshape(SHARE), right.T, right_sums.reshape(SHARE),
         operators.T, operator_state.T,
     )
+
+
+def nt(a, b):
+    return lax.dot_general(a, b, (((1,), (1,)), ((), ())), preferred_element_type=f32)
+
+
+def nn(a, b):
+    return jnp.dot(a, b, preferred_element_type=f32)
+
+
+def flag(condition):
+    return jnp.where(condition, 1.0, 0.0).astype(bf16)
+
+
+def columns(member):
+    return pl.ds(pl.multiple_of(member * SHARE, SHARE), SHARE)
+
+
+class Mail:
+    def __init__(self, send, recv):
+        self.send, self.recv, self.sent = send, recv, {}
+
+    def post(self, k, src, dst, device):
+        copy = pltpu.make_async_remote_copy(
+            src_ref=src, dst_ref=dst, send_sem=self.send.at[k], recv_sem=self.recv.at[k],
+            device_id=device, device_id_type=MESH,
+        )
+        copy.start()
+        self.sent[k] = copy
+
+    def take(self, *keys):
+        for k in keys:
+            self.sent[k].wait_recv()
+
+    def close(self):
+        for copy in self.sent.values():
+            copy.wait_send()
+
+
+class Place:
+    def __init__(self):
+        pair, edge = lax.axis_index("pair"), lax.axis_index("edge")
+        self.pair, self.edge = pair, edge
+        self.x, self.y = edge // 4, lax.rem(edge, 4)
+        self.z, self.core = pair // 4, lax.rem(pair, 2)
+        self.chip = lax.rem(pair // 2, 2) * 8 + edge
+        other = (1 - self.x) * 4
+        up, far, down = (lax.rem(self.y + d, 4) for d in (1, 2, 3))
+        self.up, self.down, self.far = self.x * 4 + up, self.x * 4 + down, self.x * 4 + far
+        self.o, self.oup, self.odown, self.ofar = other + self.y, other + up, other + down, other + far
+        self.twin = (pair + 1 - 2 * self.core, edge)
+        self.plane = []
+        for d in range(1, 16):
+            c = lax.rem(self.chip + d, 16)
+            self.plane.append((self.z * 4 + (c // 8) * 2 + self.core, lax.rem(c, 8)))
+        self.depth = [(lax.rem(pair + 4 * d, GROUPS), edge) for d in range(1, 8)]
+        self.peers = [(pair, lax.rem(edge + d, MEMBERS)) for d in range(1, MEMBERS)]
+
+    def group(self, distance):
+        return (lax.rem(self.pair + distance + GROUPS, GROUPS), self.edge)
+
+    def met(self):
+        return self.plane + self.depth + [self.twin] + [self.group(d) for d in (1, -1, 2, -2)]
+
+
+def spread(here, rows, mail):
+    up, down, far, o = here.up, here.down, here.far, here.o
+
+    def go(k, slot, piece, member):
+        ref = rows.at[piece, columns(slot)]
+        mail.post(k, ref, ref, (here.pair, member))
+
+    edge = here.edge
+    go(0, edge, A, o)
+    go(1, edge, B, far), go(2, edge, B, up), go(3, edge, B, down)
+    go(4, edge, B, o)
+    go(5, edge, A, far), go(6, edge, A, up), go(7, edge, A, down)
+    yield
+    mail.take(0)
+    go(8, o, A, far), go(9, o, A, up), go(10, o, A, down)
+    yield
+    mail.take(2)
+    go(11, down, B, o)
+    mail.take(3)
+    go(12, up, B, o)
+    mail.take(1)
+    go(13, far, B, o)
+    yield
+    mail.take(4, 5, 6, 7, 8, 9, 10, 11, 12, 13)
+    mail.close()
+
+
+def fold_scratch():
+    low = lambda *s: pltpu.VMEM(s + (SHARE,), bf16)
+    return [low(7, NA), low(7, NB), low(1, NA), low(3, NB), DMA((14,)), DMA((14,))]
+
+
+def fold(here, parts, total, land_a, land_b, out_a, out_b, send, recv):
+    mail = Mail(send, recv)
+    up, down, far, o = here.up, here.down, here.far, here.o
+
+    def go(k, src, dst, member):
+        mail.post(k, src, dst, (here.pair, member))
+
+    def part(slot, piece):
+        return parts[slot, piece].astype(f32)
+
+    for k, slot, member in ((3, here.oup, up), (4, here.odown, down), (5, here.ofar, far)):
+        go(k, parts.at[slot, A], land_a.at[k], member)
+    for k, slot in ((8, here.oup), (9, here.odown), (10, here.ofar)):
+        go(k, parts.at[slot, B], land_b.at[k - 7], o)
+    for k, slot in ((0, up), (1, down), (2, far)):
+        go(k, parts.at[slot, A], land_a.at[k], slot)
+    go(7, parts.at[o, B], land_b.at[0], o)
+    yield
+    mail.take(3, 4, 5)
+    out_a[0] = (
+        part(o, A) + land_a[3].astype(f32) + land_a[4].astype(f32) + land_a[5].astype(f32)
+    ).astype(bf16)
+    go(6, out_a.at[0], land_a.at[6], o)
+    yield
+    for i, member in enumerate((up, down, far)):
+        mail.take(8 + i)
+        out_b[i] = (part(member, B) + land_b[1 + i].astype(f32)).astype(bf16)
+        go(11 + i, out_b.at[i], land_b.at[4 + i], member)
+    yield
+    mail.take(0, 1, 2, 6)
+    total[A] = part(here.edge, A) + sum(land_a[i].astype(f32) for i in (0, 1, 2, 6))
+    mail.take(7, 11, 12, 13)
+    total[B] = part(here.edge, B) + sum(land_b[i].astype(f32) for i in (0, 4, 5, 6))
+    mail.close()
+
+
+def reduce_scratch():
+    low = lambda *s: pltpu.VMEM(s + (SHARE,), bf16)
+    return [
+        low(2, 16, 32), low(16, 32), low(16, 32), low(16, 32), low(8, 32), low(2, 16, 32),
+        DMA((2,)), DMA((2,)), DMA((15,)), DMA((15,)), DMA((7,)), DMA((7,)), DMA((15,)), DMA((15,)),
+    ]
+
+
+def reduce_all(here, share, from_twin, mine, from_plane, from_depth, whole, cs, cr, s1, r1, s2, r2, s3, r3):
+    core, chip, z = here.core, here.chip, here.z
+    twin, first, second, third = Mail(cs, cr), Mail(s1, r1), Mail(s2, r2), Mail(s3, r3)
+    twin.post(0, share.at[1 - core], from_twin, here.twin)
+    yield
+    twin.take(0)
+    mine[...] = (share[core].astype(f32) + from_twin[...].astype(f32)).astype(bf16)
+    for d, device in enumerate(here.plane):
+        first.post(d, mine.at[lax.rem(chip + d + 1, 16)], from_plane.at[chip], device)
+    yield
+    total = mine[chip].astype(f32)
+    for d in range(15):
+        first.take(d)
+        total = total + from_plane[lax.rem(chip + 15 - d, 16)].astype(f32)
+    from_depth[z] = total.astype(bf16)
+    for d, device in enumerate(here.depth):
+        second.post(d, from_depth.at[z], from_depth.at[z], device)
+    yield
+    second.take(*range(7))
+    whole[core, chip] = sum(from_depth[k].astype(f32) for k in range(8)).astype(bf16)
+    for d, device in enumerate(here.plane):
+        third.post(d, whole.at[core, chip], whole.at[core, chip], device)
+    yield
+    third.take(*range(15))
+    twin.post(1, whole.at[core], whole.at[core], here.twin)
+    yield
+    twin.take(1)
+    for mail in (twin, first, second, third):
+        mail.close()
+
+
+def update(block, state, grad):
+    state = state + jnp.sum(grad * grad, axis=0, keepdims=True) * (1.0 / D)
+    return block - ENTITY_RATE * grad / jnp.sqrt(state), state
+
+
+def draw_share(drawn):
+    picked = flag(lax.broadcasted_iota(i32, (ROWS, ROWS), 0) == drawn)
+    return nt(jnp.full((8, ROWS), 1.0, bf16), picked) * (1.0 / NEG)
+
+
+def pick(edge, ids, r, source_hot, relation_hot, target):
+    owner = jnp.concatenate(
+        [ids[m].astype(f32)[8 * r : 8 * r + 1, :] for m in range(MEMBERS)], axis=0
+    )
+    mine = owner == edge.astype(f32)
+    before = flag(
+        lax.broadcasted_iota(i32, (LANES, LANES), 0) < lax.broadcasted_iota(i32, (LANES, LANES), 1)
+    )
+    found = jnp.sum(jnp.where(mine, 1.0, 0.0), axis=1, keepdims=True)
+    starts = [jnp.zeros((1, 1), f32)]
+    for m in range(MEMBERS):
+        starts.append(starts[-1] + found[m : m + 1, :])
+    place = nn(flag(mine), before) + jnp.concatenate(starts[:MEMBERS], axis=0)
+    rank = jnp.where(mine, place, -1.0).astype(i32)
+    want = lax.broadcasted_iota(i32, (ROOM, LANES), 0)
+    as_row, as_column = jnp.zeros((16, ROOM), f32), jnp.zeros((ROOM, 16), f32)
+    for m in range(MEMBERS):
+        chosen = flag(rank[m : m + 1, :] == want)
+        as_row = as_row + nt(ids[m], chosen)
+        as_column = as_column + nt(chosen, ids[m])
+    as_row = as_row[8 * r : 8 * r + 8, :].astype(i32)
+    source_hot[...] = flag(lax.broadcasted_iota(i32, (SHARE, ROOM), 0) == as_row[1:2, :] - 1)
+    relation_hot[...] = flag(lax.broadcasted_iota(i32, (NREL, ROOM), 0) == as_row[2:3, :])
+    wanted = as_column[:, 8 * r + 3 : 8 * r + 4] * SHARE + as_column[:, 8 * r + 4 : 8 * r + 5]
+    target[...] = jnp.broadcast_to(wanted.astype(i32), (ROOM, SHARE))
+    return jnp.where(starts[MEMBERS] > ROOM, 1.0, 0.0)
+
+
+def ask(left_low, both, source_hot, relation_hot, source, operator, query, query_t):
+    source[...] = nn(left_low, source_hot[...])
+    operator[...] = nn(both[...], jnp.concatenate([relation_hot[...], relation_hot[...]], axis=0))
+    sr, si, kr, ki = source[:H], source[H:], operator[:H], operator[H:]
+    asked = jnp.concatenate([sr * kr - si * ki, sr * ki + si * kr], axis=0).astype(bf16)
+    query[...] = asked
+    query_t[...] = asked.T
+
+
+def weigh(b, rows, often, target, query_t, weight):
+    wide = pl.ds(b * 2 * SHARE, 2 * SHARE)
+    scores = nn(query_t[...], rows[:, wide])
+    lane = lax.broadcasted_iota(i32, (ROOM, SHARE), 1)
+    for j in range(2):
+        block = pl.ds((2 * b + j) * SHARE, SHARE)
+        chance = 0.5 * jnp.tanh(0.5 * scores[:, j * SHARE : (j + 1) * SHARE]) + 0.5
+        hit = lane + (2 * b + j) * SHARE == target[...]
+        value = often[0:1, block] * chance - jnp.where(hit, 1.0 - chance, 0.0)
+        weight[:, block] = value.astype(bf16)
+
+
+def right_parts(b, query, weight, parts):
+    wide = nn(query[...], weight[:, pl.ds(b * 2 * SHARE, 2 * SHARE)]).astype(bf16)
+    parts[2 * b], parts[2 * b + 1] = wide[:, :SHARE], wide[:, SHARE:]
+
+
+def train_kernel(
+    left, left_state, right, right_state, relations, relation_state,
+    source_ids, relation_ids, target_ids, sample_ids, counts,
+    left_out, left_state_out, right_out, right_state_out, relations_out, relation_state_out, missed,
+    wide, ids1, ids2, drawn1, drawn2, both, rows1, rows2, often1, often2,
+    source_hot1, relation_hot1, target1, source_hot2, relation_hot2, target2,
+    source, operator, query, query_t, weight, parts1, parts2, total, relation_sum, left_two, left_two_state,
+    out_left, in_left, out_right, in_right, out_rows, in_rows, out_states, in_states,
+    id_send, id_recv, id2_send, id2_recv, move_send, move_recv,
+    spread1_send, spread1_recv, spread2_send, spread2_recv,
+    *folds,
+):
+    fold1, fold2, reduction = folds[:6], folds[6:12], folds[12:]
+    here = Place()
+    pair, edge = here.pair, here.edge
+    barrier = pltpu.get_barrier_semaphore()
+    met = here.met()
+    for device in met:
+        pl.semaphore_signal(barrier, inc=1, device_id=device, device_id_type=MESH)
+
+    wide[...] = jnp.full_like(wide, -1.0)
+    slot = edge * SLOTS + lax.broadcasted_iota(i32, (1, SLOTS), 1)
+    for r in range(2):
+        s, k, t = (x[r : r + 1, :] for x in (source_ids, relation_ids, target_ids))
+        owner = jnp.where(slot < counts[0:1, r : r + 1], s >> 7, -1)
+        for row, value in enumerate((owner, (s & 127) + 1, k, t >> 7, t & 127)):
+            wide[8 * r + row : 8 * r + row + 1, 0:SLOTS] = value.astype(f32)
+    ids1[edge] = wide[...].astype(bf16)
+    drawn1[...] = jnp.full_like(drawn1, -1)
+    drawn1[:, 0:NEG] = sample_ids[...]
+    for j in range(8):
+        drawn2[0, j : j + 1, :] = drawn1[1:2, j * SHARE : (j + 1) * SHARE]
+    rows1[:, columns(edge)] = right[...].astype(bf16)
+    often1[...] = draw_share(drawn1[0:1, :])
+    pl.semaphore_wait(barrier, len(met))
+
+    id_mail, id2_mail, moves = Mail(id_send, id_recv), Mail(id2_send, id2_recv), Mail(move_send, move_recv)
+    ahead, behind = here.group(1), here.group(-1)
+    for d, device in enumerate(here.peers):
+        id_mail.post(d, ids1.at[edge], ids1.at[edge], device)
+    moves.post(0, ids1.at[edge], ids2.at[edge], ahead)
+    moves.post(1, drawn2.at[0], drawn2.at[1], ahead)
+    gather = spread(here, rows1, Mail(spread1_send, spread1_recv))
+    next(gather)
+    high = relations[...].astype(bf16)
+    both[:, 0:NREL] = high
+    both[:, NREL:] = (relations[...] - high.astype(f32)).astype(bf16)
+    id_mail.take(*range(7))
+    next(gather)
+    late1 = pick(edge, ids1, 0, source_hot1, relation_hot1, target1)
+    next(gather)
+    ask(left[...].astype(bf16), both, source_hot1, relation_hot1, source, operator, query, query_t)
+    moves.take(0)
+    for d, device in enumerate(here.peers):
+        id2_mail.post(d, ids2.at[edge], ids2.at[edge], device)
+    next(gather, None)
+
+    for b in range(4):
+        weigh(b, rows1, often1, target1, query_t, weight)
+        right_parts(b, query, weight, parts1)
+    folding = fold(here, parts1, total, *fold1)
+    next(folding)
+    grad = nt(rows1[...], weight[...])
+    gr, gi, kr, ki = grad[:H], grad[H:], operator[:H], operator[H:]
+    back = jnp.concatenate([gr * kr + gi * ki, gi * kr - gr * ki], axis=0).astype(bf16)
+    left_sum = nt(back, source_hot1[...])
+    block, state = update(left[...], left_state[...], left_sum)
+    out_left[...] = block.astype(bf16)
+    out_states[0] = jnp.broadcast_to(state, (8, SHARE))
+    moves.post(2, out_left, in_left, here.group(2))
+    moves.post(3, out_states.at[0], in_states.at[0], here.group(2))
+    next(folding)
+    sr, si = source[:H], source[H:]
+    back = jnp.concatenate([gr * sr + gi * si, gi * sr - gr * si], axis=0).astype(bf16)
+    relation_sum[...] = nt(back, relation_hot1[...])
+    next(folding)
+    id2_mail.take(*range(7))
+    late2 = pick(edge, ids2, 1, source_hot2, relation_hot2, target2)
+    moves.take(1)
+    often2[...] = draw_share(
+        jnp.concatenate([drawn2[1, j : j + 1, :] for j in range(8)], axis=1)
+    )
+    next(folding, None)
+    right_two, right_two_state = update(right[...], right_state[...], total[...])
+    rows2[:, columns(edge)] = right_two.astype(bf16)
+    gather = spread(here, rows2, Mail(spread2_send, spread2_recv))
+    next(gather)
+    right_out[...] = right_two
+    moves.take(2, 3)
+    left_two[...] = in_left[...].astype(f32)
+    left_two_state[...] = in_states[0, 0:1, :]
+    next(gather)
+    ask(in_left[...], both, source_hot2, relation_hot2, source, operator, query, query_t)
+    next(gather)
+    next(gather, None)
+
+    for b in range(4):
+        weigh(b, rows2, often2, target2, query_t, weight)
+    grad = nt(rows2[...], weight[...])
+    gr, gi, sr, si = grad[:H], grad[H:], source[:H], source[H:]
+    back = jnp.concatenate([gr * sr + gi * si, gi * sr - gr * si], axis=0).astype(bf16)
+    relation_grad = relation_sum[...] + nt(back, relation_hot2[...])
+    last = jnp.broadcast_to(late1 + late2, (224, SHARE))
+    share = reduction[0]
+    share[...] = (
+        jnp.concatenate([relation_grad[:, :SHARE], relation_grad[:, SHARE:], last], axis=0)
+        .reshape(2, 16, 32, SHARE)
+        .astype(bf16)
+    )
+    reducing = reduce_all(here, *reduction)
+    next(reducing)
+    for b in range(4):
+        right_parts(b, query, weight, parts2)
+    next(reducing)
+    folding = fold(here, parts2, total, *fold2)
+    next(folding)
+    kr, ki = operator[:H], operator[H:]
+    back = jnp.concatenate([gr * kr + gi * ki, gi * kr - gr * ki], axis=0).astype(bf16)
+    left_sum = nt(back, source_hot2[...])
+    block, state = update(left_two[...], left_two_state[...], left_sum)
+    out_rows[0] = block.astype(bf16)
+    out_states[1] = jnp.broadcast_to(state, (8, SHARE))
+    moves.post(4, out_rows.at[0], in_rows.at[0], behind)
+    moves.post(5, out_states.at[1], in_states.at[1], behind)
+    next(folding)
+    next(reducing)
+    next(folding)
+    next(folding, None)
+    block, state = update(right_two, right_two_state, total[...])
+    out_rows[1] = block.astype(bf16)
+    out_states[2] = jnp.broadcast_to(state, (8, SHARE))
+    moves.post(6, out_rows.at[1], in_rows.at[1], behind)
+    moves.post(7, out_states.at[2], in_states.at[2], behind)
+    next(reducing)
+    moves.take(4, 5)
+    left_out[...] = in_rows[0].astype(f32)
+    left_state_out[...] = in_states[1, 0:1, :]
+    next(reducing)
+    moves.take(6, 7)
+    right_out[...] = in_rows[1].astype(f32)
+    right_state_out[...] = in_states[2, 0:1, :]
+    next(reducing, None)
+    whole = reduction[5]
+    gathered = whole[...].reshape(ROWS, SHARE).astype(f32)
+    grad = jnp.concatenate([gathered[0:D], gathered[D : 2 * D]], axis=1)
+    state = relation_state[...] + grad * grad
+    relation_state_out[...] = state
+    relations_out[...] = relations[...] - RELATION_RATE * grad / jnp.sqrt(state)
+    missed[...] = gathered[2 * D : 2 * D + 8]
+    for mail in (id_mail, id2_mail, moves):
+        mail.close()
+
+
+def train(*args):
+    table = jax.ShapeDtypeStruct((D, NREL), f32)
+    block = jax.ShapeDtypeStruct((D, SHARE), f32)
+    row = jax.ShapeDtypeStruct((1, SHARE), f32)
+    vmem = pltpu.VMEM
+    low = vmem((D, SHARE), bf16)
+    hots = [vmem((SHARE, ROOM), bf16), vmem((NREL, ROOM), bf16), vmem((ROOM, SHARE), i32)]
+    return pl.pallas_call(
+        train_kernel,
+        out_shape=(block, row, block, row, table, table, jax.ShapeDtypeStruct((8, SHARE), f32)),
+        in_specs=[VMEM] * 11,
+        out_specs=(VMEM,) * 7,
+        scratch_shapes=[
+            vmem((16, LANES), f32),
+            vmem((MEMBERS, 16, LANES), bf16), vmem((MEMBERS, 16, LANES), bf16),
+            vmem((2, ROWS), i32), vmem((2, 8, SHARE), i32),
+            vmem((D, 2 * NREL), bf16),
+            vmem((D, ROWS), bf16), vmem((D, ROWS), bf16),
+            vmem((8, ROWS), f32), vmem((8, ROWS), f32),
+            *hots, *hots,
+            vmem((D, ROOM), f32), vmem((D, ROOM), f32),
+            vmem((D, ROOM), bf16), vmem((ROOM, D), bf16), vmem((ROOM, ROWS), bf16),
+            vmem((MEMBERS, D, SHARE), bf16), vmem((MEMBERS, D, SHARE), bf16),
+            vmem((D, SHARE), f32), vmem((D, NREL), f32),
+            vmem((D, SHARE), f32), vmem((1, SHARE), f32),
+            low, low, low, low, vmem((2, D, SHARE), bf16), vmem((2, D, SHARE), bf16),
+            vmem((3, 8, SHARE), f32), vmem((3, 8, SHARE), f32),
+            DMA((7,)), DMA((7,)), DMA((7,)), DMA((7,)), DMA((8,)), DMA((8,)),
+            DMA((14,)), DMA((14,)), DMA((14,)), DMA((14,)),
+            *fold_scratch(), *fold_scratch(), *reduce_scratch(),
+        ],
+        compiler_params=pltpu.CompilerParams(
+            collective_id=1, has_side_effects=True, vmem_limit_bytes=56 * 2**20
+        ),
+        name="train_two_rounds",
+    )(*args)
+
+
+def settle_kernel(*refs):
+    for given, out in zip(refs[:6], refs[6:]):
+        out[...] = given[...]
+
+
+def settle(done):
+    left, left_sums, right, right_sums, table, table_state = done
+    flat = (left.T, left_sums.reshape(1, SHARE), right.T, right_sums.reshape(1, SHARE), table.T, table_state.T)
+    left, left_sums, right, right_sums, table, table_state = pl.pallas_call(
+        settle_kernel,
+        out_shape=tuple(jax.ShapeDtypeStruct(x.shape, x.dtype) for x in flat),
+        in_specs=[VMEM] * 6,
+        out_specs=(VMEM,) * 6,
+        name="settle",
+    )(*flat)
+    return (
+        left.T, left_sums.reshape(SHARE), right.T, right_sums.reshape(SHARE), table.T, table_state.T,
+    )
+
+
+def body(
+    left_block, left_state, right_block, right_state, relations, relation_state,
+    source_ids, relation_ids, target_ids, sample_ids, bucket_counts,
+):
+    left, left_sums, right, right_sums, table, table_state, missed = train(
+        left_block.T, left_state.reshape(1, SHARE), right_block.T, right_state.reshape(1, SHARE),
+        relations.T, relation_state.T,
+        source_ids, relation_ids, target_ids, sample_ids, bucket_counts.T,
+    )
+    fast = (
+        left.T, left_sums.reshape(SHARE), right.T, right_sums.reshape(SHARE), table.T, table_state.T,
+    )
+    done = lax.cond(
+        missed[0, 0] > 0.0,
+        lambda *args: any_spread(*args[6:]),
+        lambda *args: args[:6],
+        *fast,
+        left_block, left_state, right_block, right_state, relations, relation_state,
+        source_ids, relation_ids, target_ids, sample_ids, bucket_counts,
+    )
+    return settle(done)
 
 
 def solution(mesh):

time: 109 us -> 77.8 us (0.71); the launches traced: 107 us -> 77.6 us
  Pallas kernels: 99.3 us -> 74.2 us
  local copies, waits for them, and re-layouts: 7.09 us -> 1.9 us
    pallas_call x5 -> x2, Pallas kernels: 99.3 us -> 74.2 us  [the longest x1 73.1 us: train(): pl.pallas_call(train_kernel, out_shape=(block, row, block, row, table, ta...]
    unnamed x23 -> x22, local copies, waits for them, and re-layouts: 7.06 us -> 0.7 us
    slice x0 -> x1, local copies, waits for them, and re-layouts: none -> 1.2 us  [body(): missed[0, 0] > 0.0]
where the time goes in v2:
time: 77.8 us; the launch traced here: 77.6 us
  Pallas kernels  74.2 us (95%)
  local copies, waits for them, and re-layouts  1.9 us (2%)
  between operations  1.44 us (2%)
    pallas_call x1, Pallas kernels, train(): pl.pallas_call(train_kernel, out_shape=(block, row, block, row, table, ta...  73.1 us

profile of v2, /device:TPU:1, one launch (start us, length us, event | category | flops | bytes accessed | tf_op | source)
XLA Modules:
  0.0 77.6 jit_solution(4412023046691659782)
XLA Ops:
  0.6 0.0 copy-start.6
  0.6 0.0 copy-start.7
  0.7 0.0 copy-start.10
  0.7 0.0 copy-start.11
  0.7 0.0 copy-start.12
  0.7 0.6 copy-done.6
  1.3 0.0 copy-done.7
  1.3 0.0 copy-done.10
  1.3 0.0 copy-done.11
  1.3 0.0 copy-done.12
  1.4 0.0 copy-start.2
  1.4 0.0 copy-start.3
  1.4 0.0 copy-start.4
  1.4 0.0 copy-start.5
  1.4 73.1 %train_two_rounds.1 = (f32[400,128]{1,0:T(8,128)S(1)}, f32[1,128]{1,0:T(1,128)S(1)}, f32[400,128]{1,0:T(8,128)S(1)}, f32[1,128]{1,0:T(1,128)S(1)}, f32[400,256]{...) custom-call(f32[400,128]{1,0:T(8,128)} %bitcast.41, f32[1,128]{1,0:T(1,128)S(1)} %bitcast.57, ...), custom_call_target="tpu_custom_call" | custom-call | tf_op jit(solution)/shard_map/train_two_rounds/pallas_call | solution.py:805
  74.5 0.0 copy-start.9
  74.5 1.2 %slice.3 = f32[1,1]{1,0:T(1,128)} slice(f32[8,128]{1,0:T(8,128)} %get-tuple-element.99), slice={[0:1], [0:1]} | slice | bytes 8 | tf_op jit(solution)/shard_map/slice | solution.py:869
  75.7 0.0 copy-start.8
  76.4 0.0 copy-done.2
  76.4 0.0 copy-done.3
  76.4 0.0 copy-done.4
  76.4 0.0 copy-done.5
  76.4 0.0 copy-done.9
  76.4 0.0 copy-done.8
  76.5 1.1 %settle.1 = (f32[400,128]{1,0:T(8,128)}, f32[1,128]{1,0:T(1,128)}, f32[400,128]{1,0:T(8,128)}, f32[1,128]{1,0:T(1,128)}, f32[400,256]{1,0:T(8,128)}, /*index=5*/f32[400,256]{1,0:T(8,128)}) custom-call(f32[400,128]{1,0:T(8,128)S(1)} %bitcast.54, f32[1,128]{1,0:T(1,128)S(1)} %get-tuple-element.107.refs_1_, f32[400,128]{1,0:T(8,128)S(1)} %bitcast.51, ...), custom_call_target="tpu_custom_call" | custom-call | tf_op jit(solution)/shard_map/settle/pallas_call | solution.py:844
  (1 shorter events, 0.0 us)
Async XLA Ops:
  0.6 0.7 copy-start.6
  0.6 0.7 copy-start.7
  0.7 0.7 copy-start.10
  0.7 0.7 copy-start.11
  0.7 0.7 copy-start.12
  1.4 75.0 %copy-start.2 = (f32[256,400]{0,1:T(8,128)S(1)}, f32[256,400]{0,1:T(8,128)}, u32[]{:S(2)}) copy-start(f32[256,400]{0,1:T(8,128)} %param.17) | copy-start | bytes 1228804
  1.4 75.0 %copy-start.3 = (f32[128,400]{0,1:T(8,128)S(1)}, f32[128,400]{0,1:T(8,128)}, u32[]{:S(2)}) copy-start(f32[128,400]{0,1:T(8,128)} %param.15) | copy-start | bytes 614404
  1.4 75.0 %copy-start.4 = (f32[256,400]{0,1:T(8,128)S(1)}, f32[256,400]{0,1:T(8,128)}, u32[]{:S(2)}) copy-start(f32[256,400]{0,1:T(8,128)} %param.18) | copy-start | bytes 1228804
  1.4 75.0 %copy-start.5 = (f32[128,400]{0,1:T(8,128)S(1)}, f32[128,400]{0,1:T(8,128)}, u32[]{:S(2)}) copy-start(f32[128,400]{0,1:T(8,128)} %param.13) | copy-start | bytes 614404
  74.5 1.9 %copy-start.9 = (s32[2,500]{1,0:T(2,128)S(1)}, s32[2,500]{1,0:T(2,128)}, u32[]{:S(2)}) copy-start(s32[2,500]{1,0:T(2,128)} %target_ids.1) | copy-start | bytes 12004
  75.7 0.7 copy-start.8

commit v3 on v2

--- a/solution.py
+++ b/solution.py
@@ -452,10 +452,8 @@
         self.x, self.y = edge // 4, lax.rem(edge, 4)
         self.z, self.core = pair // 4, lax.rem(pair, 2)
         self.chip = lax.rem(pair // 2, 2) * 8 + edge
-        other = (1 - self.x) * 4
-        up, far, down = (lax.rem(self.y + d, 4) for d in (1, 2, 3))
-        self.up, self.down, self.far = self.x * 4 + up, self.x * 4 + down, self.x * 4 + far
-        self.o, self.oup, self.odown, self.ofar = other + self.y, other + up, other + down, other + far
+        self.up, self.far, self.down = (lax.rem(self.y + d, 4) for d in (1, 2, 3))
+        self.o, self.oup, self.ofar, self.odown = (4 + v for v in (self.y, self.up, self.far, self.down))
         self.twin = (pair + 1 - 2 * self.core, edge)
         self.plane = []
         for d in range(1, 16):
@@ -467,6 +465,9 @@
     def group(self, distance):
         return (lax.rem(self.pair + distance + GROUPS, GROUPS), self.edge)
 
+    def member(self, slot):
+        return (self.pair, lax.rem(slot + 4 * self.x, MEMBERS))
+
     def met(self):
         return self.plane + self.depth + [self.twin] + [self.group(d) for d in (1, -1, 2, -2)]
 
@@ -474,15 +475,15 @@
 def spread(here, rows, mail):
     up, down, far, o = here.up, here.down, here.far, here.o
 
-    def go(k, slot, piece, member):
-        ref = rows.at[piece, columns(slot)]
-        mail.post(k, ref, ref, (here.pair, member))
-
-    edge = here.edge
-    go(0, edge, A, o)
-    go(1, edge, B, far), go(2, edge, B, up), go(3, edge, B, down)
-    go(4, edge, B, o)
-    go(5, edge, A, far), go(6, edge, A, up), go(7, edge, A, down)
+    def go(k, slot, piece, to):
+        there = lax.rem(slot + 4, MEMBERS) if to is o else slot
+        mail.post(k, rows.at[piece, columns(slot)], rows.at[piece, columns(there)], here.member(to))
+
+    me = here.y
+    go(0, me, A, o)
+    go(1, me, B, far), go(2, me, B, up), go(3, me, B, down)
+    go(4, me, B, o)
+    go(5, me, A, far), go(6, me, A, up), go(7, me, A, down)
     yield
     mail.take(0)
     go(8, o, A, far), go(9, o, A, up), go(10, o, A, down)
@@ -491,10 +492,13 @@
     go(11, down, B, o)
     mail.take(3)
     go(12, up, B, o)
+    yield
     mail.take(1)
     go(13, far, B, o)
     yield
-    mail.take(4, 5, 6, 7, 8, 9, 10, 11, 12, 13)
+    mail.take(5, 6, 7)
+    yield
+    mail.take(4, 8, 9, 10, 11, 12, 13)
     mail.close()
 
 
@@ -507,18 +511,19 @@
     mail = Mail(send, recv)
     up, down, far, o = here.up, here.down, here.far, here.o
 
-    def go(k, src, dst, member):
-        mail.post(k, src, dst, (here.pair, member))
+    def go(k, src, dst, to):
+        mail.post(k, src, dst, here.member(to))
 
     def part(slot, piece):
         return parts[slot, piece].astype(f32)
 
-    for k, slot, member in ((3, here.oup, up), (4, here.odown, down), (5, here.ofar, far)):
+    for k, slot in ((2, far), (0, up), (1, down)):
+        go(k, parts.at[slot, A], land_a.at[k], slot)
+    yield
+    for k, slot, member in ((5, here.ofar, far), (3, here.oup, up), (4, here.odown, down)):
         go(k, parts.at[slot, A], land_a.at[k], member)
-    for k, slot in ((8, here.oup), (9, here.odown), (10, here.ofar)):
+    for k, slot in ((10, here.ofar), (8, here.oup), (9, here.odown)):
         go(k, parts.at[slot, B], land_b.at[k - 7], o)
-    for k, slot in ((0, up), (1, down), (2, far)):
-        go(k, parts.at[slot, A], land_a.at[k], slot)
     go(7, parts.at[o, B], land_b.at[0], o)
     yield
     mail.take(3, 4, 5)
@@ -527,15 +532,15 @@
     ).astype(bf16)
     go(6, out_a.at[0], land_a.at[6], o)
     yield
-    for i, member in enumerate((up, down, far)):
+    for i, member in ((2, far), (0, up), (1, down)):
         mail.take(8 + i)
         out_b[i] = (part(member, B) + land_b[1 + i].astype(f32)).astype(bf16)
         go(11 + i, out_b.at[i], land_b.at[4 + i], member)
     yield
     mail.take(0, 1, 2, 6)
-    total[A] = part(here.edge, A) + sum(land_a[i].astype(f32) for i in (0, 1, 2, 6))
+    total[A] = part(here.y, A) + sum(land_a[i].astype(f32) for i in (0, 1, 2, 6))
     mail.take(7, 11, 12, 13)
-    total[B] = part(here.edge, B) + sum(land_b[i].astype(f32) for i in (0, 4, 5, 6))
+    total[B] = part(here.y, B) + sum(land_b[i].astype(f32) for i in (0, 4, 5, 6))
     mail.close()
 
 
@@ -543,7 +548,7 @@
     low = lambda *s: pltpu.VMEM(s + (SHARE,), bf16)
     return [
         low(2, 16, 32), low(16, 32), low(16, 32), low(16, 32), low(8, 32), low(2, 16, 32),
-        DMA((2,)), DMA((2,)), DMA((15,)), DMA((15,)), DMA((7,)), DMA((7,)), DMA((15,)), DMA((15,)),
+        DMA((17,)), DMA((17,)), DMA((15,)), DMA((15,)), DMA((7,)), DMA((7,)), DMA((15,)), DMA((15,)),
     ]
 
 
@@ -569,11 +574,14 @@
     whole[core, chip] = sum(from_depth[k].astype(f32) for k in range(8)).astype(bf16)
     for d, device in enumerate(here.plane):
         third.post(d, whole.at[core, chip], whole.at[core, chip], device)
-    yield
-    third.take(*range(15))
-    twin.post(1, whole.at[core], whole.at[core], here.twin)
-    yield
-    twin.take(1)
+    twin.post(16, whole.at[core, chip], whole.at[core, chip], here.twin)
+    yield
+    for d in range(15):
+        third.take(d)
+        chunk = whole.at[core, lax.rem(chip + 15 - d, 16)]
+        twin.post(1 + d, chunk, chunk, here.twin)
+    yield
+    twin.take(*range(1, 17))
     for mail in (twin, first, second, third):
         mail.close()
 
@@ -583,12 +591,13 @@
     return block - ENTITY_RATE * grad / jnp.sqrt(state), state
 
 
-def draw_share(drawn):
+def draw_share(x, drawn):
+    drawn = jnp.where(drawn < 0, -1, (drawn + 4 * SHARE * x) & (ROWS - 1))
     picked = flag(lax.broadcasted_iota(i32, (ROWS, ROWS), 0) == drawn)
     return nt(jnp.full((8, ROWS), 1.0, bf16), picked) * (1.0 / NEG)
 
 
-def pick(edge, ids, r, source_hot, relation_hot, target):
+def line_up(edge, ids, r):
     owner = jnp.concatenate(
         [ids[m].astype(f32)[8 * r : 8 * r + 1, :] for m in range(MEMBERS)], axis=0
     )
@@ -602,18 +611,30 @@
         starts.append(starts[-1] + found[m : m + 1, :])
     place = nn(flag(mine), before) + jnp.concatenate(starts[:MEMBERS], axis=0)
     rank = jnp.where(mine, place, -1.0).astype(i32)
-    want = lax.broadcasted_iota(i32, (ROOM, LANES), 0)
-    as_row, as_column = jnp.zeros((16, ROOM), f32), jnp.zeros((ROOM, 16), f32)
+    return rank, jnp.where(starts[MEMBERS] > ROOM, 1.0, 0.0)
+
+
+def pick(x, rank, ids, r, source_hot, relation_hot, target):
+    high, low = rank >> 7, rank & (SHARE - 1)
+    as_row, as_column = jnp.zeros((32, SHARE), f32), jnp.zeros((SHARE, 32), f32)
     for m in range(MEMBERS):
-        chosen = flag(rank[m : m + 1, :] == want)
-        as_row = as_row + nt(ids[m], chosen)
-        as_column = as_column + nt(chosen, ids[m])
-    as_row = as_row[8 * r : 8 * r + 8, :].astype(i32)
-    source_hot[...] = flag(lax.broadcasted_iota(i32, (SHARE, ROOM), 0) == as_row[1:2, :] - 1)
-    relation_hot[...] = flag(lax.broadcasted_iota(i32, (NREL, ROOM), 0) == as_row[2:3, :])
-    wanted = as_column[:, 8 * r + 3 : 8 * r + 4] * SHARE + as_column[:, 8 * r + 4 : 8 * r + 5]
-    target[...] = jnp.broadcast_to(wanted.astype(i32), (ROOM, SHARE))
-    return jnp.where(starts[MEMBERS] > ROOM, 1.0, 0.0)
+        low_hot = flag(lax.broadcasted_iota(i32, (SHARE, LANES), 0) == low[m : m + 1, :])
+        high_hot = lax.broadcasted_iota(i32, (8, LANES), 0) == high[m : m + 1, :]
+        values = ids[m].astype(f32)[8 * r : 8 * r + 8]
+        values = jnp.concatenate(
+            [jnp.where(high_hot, values[f : f + 1, :], 0.0) for f in range(1, 5)], axis=0
+        ).astype(bf16)
+        as_row = as_row + nt(values, low_hot)
+        as_column = as_column + nt(low_hot, values)
+    blocks = range(ROOM // SHARE)
+    s = jnp.concatenate([as_row[h : h + 1, :] for h in blocks], axis=1).astype(i32)
+    k = jnp.concatenate([as_row[8 + h : 9 + h, :] for h in blocks], axis=1).astype(i32)
+    source_hot[...] = flag(lax.broadcasted_iota(i32, (SHARE, ROOM), 0) == s - 1)
+    relation_hot[...] = flag(lax.broadcasted_iota(i32, (NREL, ROOM), 0) == k)
+    wanted = as_column.astype(i32)
+    for h in blocks:
+        t = ((wanted[:, 16 + h : 17 + h] + 4 * x) & 7) * SHARE + wanted[:, 24 + h : 25 + h]
+        target[h * SHARE : (h + 1) * SHARE, :] = jnp.broadcast_to(t, (SHARE, SHARE))
 
 
 def ask(left_low, both, source_hot, relation_hot, source, operator, query, query_t):
@@ -625,24 +646,39 @@
     query_t[...] = asked.T
 
 
-def weigh(b, rows, often, target, query_t, weight):
-    wide = pl.ds(b * 2 * SHARE, 2 * SHARE)
-    scores = nn(query_t[...], rows[:, wide])
+def weigh(half, rows, often, target, query_t, weight):
     lane = lax.broadcasted_iota(i32, (ROOM, SHARE), 1)
-    for j in range(2):
-        block = pl.ds((2 * b + j) * SHARE, SHARE)
-        chance = 0.5 * jnp.tanh(0.5 * scores[:, j * SHARE : (j + 1) * SHARE]) + 0.5
-        hit = lane + (2 * b + j) * SHARE == target[...]
-        value = often[0:1, block] * chance - jnp.where(hit, 1.0 - chance, 0.0)
-        weight[:, block] = value.astype(bf16)
-
-
-def right_parts(b, query, weight, parts):
-    wide = nn(query[...], weight[:, pl.ds(b * 2 * SHARE, 2 * SHARE)]).astype(bf16)
-    parts[2 * b], parts[2 * b + 1] = wide[:, :SHARE], wide[:, SHARE:]
+    for b in range(2):
+        start = (4 * half + 2 * b) * SHARE
+        scores = nn(query_t[...], rows[:, pl.ds(start, 2 * SHARE)])
+        for j in range(2):
+            block = pl.ds(start + j * SHARE, SHARE)
+            chance = 0.5 * jnp.tanh(0.5 * scores[:, j * SHARE : (j + 1) * SHARE]) + 0.5
+            hit = lane + (start + j * SHARE) == target[...]
+            value = often[0:1, block] * chance - jnp.where(hit, 1.0 - chance, 0.0)
+            weight[:, block] = value.astype(bf16)
+
+
+def right_parts(half, query, weight, parts):
+    for b in range(2):
+        first = 4 * half + 2 * b
+        wide = nn(query[...], weight[:, pl.ds(first * SHARE, 2 * SHARE)]).astype(bf16)
+        parts[first], parts[first + 1] = wide[:, :SHARE], wide[:, SHARE:]
 
 
 def train_kernel(
+    *refs,
+):
+    fetched, loads = refs[18:29], refs[29]
+    fetch = [
+        pltpu.make_async_copy(given, taken, loads.at[i])
+        for i, (given, taken) in enumerate(zip(refs[:11], fetched))
+    ]
+    train_rounds(fetch, *fetched, *refs[11:18], *refs[30:])
+
+
+def train_rounds(
+    fetch,
     left, left_state, right, right_state, relations, relation_state,
     source_ids, relation_ids, target_ids, sample_ids, counts,
     left_out, left_state_out, right_out, right_state_out, relations_out, relation_state_out, missed,
@@ -655,6 +691,8 @@
     *folds,
 ):
     fold1, fold2, reduction = folds[:6], folds[6:12], folds[12:]
+    for i in (6, 7, 8, 10, 2, 9, 4, 0, 1, 3, 5):
+        fetch[i].start()
     here = Place()
     pair, edge = here.pair, here.edge
     barrier = pltpu.get_barrier_semaphore()
@@ -663,6 +701,8 @@
         pl.semaphore_signal(barrier, inc=1, device_id=device, device_id_type=MESH)
 
     wide[...] = jnp.full_like(wide, -1.0)
+    for i in (6, 7, 8, 10):
+        fetch[i].wait()
     slot = edge * SLOTS + lax.broadcasted_iota(i32, (1, SLOTS), 1)
     for r in range(2):
         s, k, t = (x[r : r + 1, :] for x in (source_ids, relation_ids, target_ids))
@@ -670,40 +710,51 @@
         for row, value in enumerate((owner, (s & 127) + 1, k, t >> 7, t & 127)):
             wide[8 * r + row : 8 * r + row + 1, 0:SLOTS] = value.astype(f32)
     ids1[edge] = wide[...].astype(bf16)
+    fetch[2].wait()
+    rows1[:, columns(here.y)] = right[...].astype(bf16)
+    pl.semaphore_wait(barrier, len(met))
+
+    id_mail, id2_mail, moves = Mail(id_send, id_recv), Mail(id2_send, id2_recv), Mail(move_send, move_recv)
+    ahead, behind = here.group(1), here.group(-1)
+    for d, device in enumerate(here.peers):
+        id_mail.post(d, ids1.at[edge], ids1.at[edge], device)
+    gather = spread(here, rows1, Mail(spread1_send, spread1_recv))
+    next(gather)
+    moves.post(0, ids1.at[edge], ids2.at[edge], ahead)
+    fetch[9].wait()
     drawn1[...] = jnp.full_like(drawn1, -1)
     drawn1[:, 0:NEG] = sample_ids[...]
     for j in range(8):
         drawn2[0, j : j + 1, :] = drawn1[1:2, j * SHARE : (j + 1) * SHARE]
-    rows1[:, columns(edge)] = right[...].astype(bf16)
-    often1[...] = draw_share(drawn1[0:1, :])
-    pl.semaphore_wait(barrier, len(met))
-
-    id_mail, id2_mail, moves = Mail(id_send, id_recv), Mail(id2_send, id2_recv), Mail(move_send, move_recv)
-    ahead, behind = here.group(1), here.group(-1)
-    for d, device in enumerate(here.peers):
-        id_mail.post(d, ids1.at[edge], ids1.at[edge], device)
-    moves.post(0, ids1.at[edge], ids2.at[edge], ahead)
     moves.post(1, drawn2.at[0], drawn2.at[1], ahead)
-    gather = spread(here, rows1, Mail(spread1_send, spread1_recv))
-    next(gather)
+    often1[...] = draw_share(here.x, drawn1[0:1, :])
+    fetch[4].wait()
     high = relations[...].astype(bf16)
     both[:, 0:NREL] = high
     both[:, NREL:] = (relations[...] - high.astype(f32)).astype(bf16)
+    next(gather)
     id_mail.take(*range(7))
+    rank, late1 = line_up(edge, ids1, 0)
     next(gather)
-    late1 = pick(edge, ids1, 0, source_hot1, relation_hot1, target1)
     next(gather)
+    pick(here.x, rank, ids1, 0, source_hot1, relation_hot1, target1)
+    fetch[0].wait()
     ask(left[...].astype(bf16), both, source_hot1, relation_hot1, source, operator, query, query_t)
     moves.take(0)
     for d, device in enumerate(here.peers):
         id2_mail.post(d, ids2.at[edge], ids2.at[edge], device)
-    next(gather, None)
-
-    for b in range(4):
-        weigh(b, rows1, often1, target1, query_t, weight)
-        right_parts(b, query, weight, parts1)
+    next(gather)
+
+    weigh(0, rows1, often1, target1, query_t, weight)
+    right_parts(0, query, weight, parts1)
     folding = fold(here, parts1, total, *fold1)
     next(folding)
+    next(gather, None)
+    weigh(1, rows1, often1, target1, query_t, weight)
+    right_parts(1, query, weight, parts1)
+    next(folding)
+    for i in (1, 3, 5):
+        fetch[i].wait()
     grad = nt(rows1[...], weight[...])
     gr, gi, kr, ki = grad[:H], grad[H:], operator[:H], operator[H:]
     back = jnp.concatenate([gr * kr + gi * ki, gi * kr - gr * ki], axis=0).astype(bf16)
@@ -716,48 +767,49 @@
     next(folding)
     sr, si = source[:H], source[H:]
     back = jnp.concatenate([gr * sr + gi * si, gi * sr - gr * si], axis=0).astype(bf16)
-    relation_sum[...] = nt(back, relation_hot1[...])
+    for c in range(2):
+        relation_sum[c] = nt(back, relation_hot1[c * SHARE : (c + 1) * SHARE, :])
     next(folding)
     id2_mail.take(*range(7))
-    late2 = pick(edge, ids2, 1, source_hot2, relation_hot2, target2)
+    rank, late2 = line_up(edge, ids2, 1)
+    pick(here.x, rank, ids2, 1, source_hot2, relation_hot2, target2)
     moves.take(1)
     often2[...] = draw_share(
-        jnp.concatenate([drawn2[1, j : j + 1, :] for j in range(8)], axis=1)
+        here.x, jnp.concatenate([drawn2[1, j : j + 1, :] for j in range(8)], axis=1)
     )
     next(folding, None)
     right_two, right_two_state = update(right[...], right_state[...], total[...])
-    rows2[:, columns(edge)] = right_two.astype(bf16)
+    rows2[:, columns(here.y)] = right_two.astype(bf16)
     gather = spread(here, rows2, Mail(spread2_send, spread2_recv))
     next(gather)
-    right_out[...] = right_two
     moves.take(2, 3)
     left_two[...] = in_left[...].astype(f32)
     left_two_state[...] = in_states[0, 0:1, :]
-    next(gather)
     ask(in_left[...], both, source_hot2, relation_hot2, source, operator, query, query_t)
-    next(gather)
+    for _ in range(4):
+        next(gather)
+
+    weigh(0, rows2, often2, target2, query_t, weight)
+    right_parts(0, query, weight, parts2)
+    folding = fold(here, parts2, total, *fold2)
+    next(folding)
     next(gather, None)
-
-    for b in range(4):
-        weigh(b, rows2, often2, target2, query_t, weight)
+    weigh(1, rows2, often2, target2, query_t, weight)
     grad = nt(rows2[...], weight[...])
     gr, gi, sr, si = grad[:H], grad[H:], source[:H], source[H:]
     back = jnp.concatenate([gr * sr + gi * si, gi * sr - gr * si], axis=0).astype(bf16)
-    relation_grad = relation_sum[...] + nt(back, relation_hot2[...])
-    last = jnp.broadcast_to(late1 + late2, (224, SHARE))
-    share = reduction[0]
-    share[...] = (
-        jnp.concatenate([relation_grad[:, :SHARE], relation_grad[:, SHARE:], last], axis=0)
-        .reshape(2, 16, 32, SHARE)
-        .astype(bf16)
-    )
+    last = jnp.broadcast_to(late1 + late2, (512 - D, SHARE))
+    share, whole = reduction[0], reduction[5]
     reducing = reduce_all(here, *reduction)
+    for c in (1 - here.core, here.core):
+        hot = relation_hot2[columns(c), :]
+        full = jnp.concatenate([relation_sum[c] + nt(back, hot), last], axis=0)
+        share[c] = full.reshape(16, 32, SHARE).astype(bf16)
+        if c is not here.core:
+            next(reducing)
+    right_parts(1, query, weight, parts2)
+    next(folding)
     next(reducing)
-    for b in range(4):
-        right_parts(b, query, weight, parts2)
-    next(reducing)
-    folding = fold(here, parts2, total, *fold2)
-    next(folding)
     kr, ki = operator[:H], operator[H:]
     back = jnp.concatenate([gr * kr + gi * ki, gi * kr - gr * ki], axis=0).astype(bf16)
     left_sum = nt(back, source_hot2[...])
@@ -769,28 +821,32 @@
     next(folding)
     next(reducing)
     next(folding)
+    next(reducing)
     next(folding, None)
     block, state = update(right_two, right_two_state, total[...])
     out_rows[1] = block.astype(bf16)
     out_states[2] = jnp.broadcast_to(state, (8, SHARE))
     moves.post(6, out_rows.at[1], in_rows.at[1], behind)
     moves.post(7, out_states.at[2], in_states.at[2], behind)
-    next(reducing)
     moves.take(4, 5)
     left_out[...] = in_rows[0].astype(f32)
     left_state_out[...] = in_states[1, 0:1, :]
     next(reducing)
+
+    def relation_update(c):
+        half = columns(c)
+        grad = whole[c].reshape(512, SHARE)[:D].astype(f32)
+        state = relation_state[:, half] + grad * grad
+        relation_state_out[:, half] = state
+        relations_out[:, half] = relations[:, half] - RELATION_RATE * grad / jnp.sqrt(state)
+
+    relation_update(here.core)
+    missed[...] = whole[here.core].reshape(512, SHARE)[D : D + 16].astype(f32)[0:1, 0:1].astype(i32)
     moves.take(6, 7)
     right_out[...] = in_rows[1].astype(f32)
     right_state_out[...] = in_states[2, 0:1, :]
     next(reducing, None)
-    whole = reduction[5]
-    gathered = whole[...].reshape(ROWS, SHARE).astype(f32)
-    grad = jnp.concatenate([gathered[0:D], gathered[D : 2 * D]], axis=1)
-    state = relation_state[...] + grad * grad
-    relation_state_out[...] = state
-    relations_out[...] = relations[...] - RELATION_RATE * grad / jnp.sqrt(state)
-    missed[...] = gathered[2 * D : 2 * D + 8]
+    relation_update(1 - here.core)
     for mail in (id_mail, id2_mail, moves):
         mail.close()
 
@@ -804,10 +860,11 @@
     hots = [vmem((SHARE, ROOM), bf16), vmem((NREL, ROOM), bf16), vmem((ROOM, SHARE), i32)]
     return pl.pallas_call(
         train_kernel,
-        out_shape=(block, row, block, row, table, table, jax.ShapeDtypeStruct((8, SHARE), f32)),
-        in_specs=[VMEM] * 11,
+        out_shape=(block, row, block, row, table, table, jax.ShapeDtypeStruct((1, 1), i32)),
+        in_specs=[pl.BlockSpec(memory_space=pl.ANY)] * 11,
         out_specs=(VMEM,) * 7,
         scratch_shapes=[
+            *(vmem(x.shape, x.dtype) for x in args), DMA((11,)),
             vmem((16, LANES), f32),
             vmem((MEMBERS, 16, LANES), bf16), vmem((MEMBERS, 16, LANES), bf16),
             vmem((2, ROWS), i32), vmem((2, 8, SHARE), i32),
@@ -818,7 +875,7 @@
             vmem((D, ROOM), f32), vmem((D, ROOM), f32),
             vmem((D, ROOM), bf16), vmem((ROOM, D), bf16), vmem((ROOM, ROWS), bf16),
             vmem((MEMBERS, D, SHARE), bf16), vmem((MEMBERS, D, SHARE), bf16),
-            vmem((D, SHARE), f32), vmem((D, NREL), f32),
+            vmem((D, SHARE), f32), vmem((2, D, SHARE), f32),
             vmem((D, SHARE), f32), vmem((1, SHARE), f32),
             low, low, low, low, vmem((2, D, SHARE), bf16), vmem((2, D, SHARE), bf16),
             vmem((3, 8, SHARE), f32), vmem((3, 8, SHARE), f32),
@@ -866,7 +923,7 @@
         left.T, left_sums.reshape(SHARE), right.T, right_sums.reshape(SHARE), table.T, table_state.T,
     )
     done = lax.cond(
-        missed[0, 0] > 0.0,
+        missed[0, 0] > 0,
         lambda *args: any_spread(*args[6:]),
         lambda *args: args[:6],
         *fast,

time: 77.8 us -> 74.8 us (0.961)
  Pallas kernels: 74.2 us -> 71.8 us
    pallas_call x1, Pallas kernels: 73.1 us -> 70.7 us  [train(): pl.pallas_call(train_kernel, out_shape=(block, row, block, row, table, ta...]
    slice x1 -> x0, local copies, waits for them, and re-layouts: 1.2 us -> none  [body(): missed[0, 0] > 0.0]
where the time goes in v3:
time: 74.8 us; the launch traced here: 74.6 us
  Pallas kernels  71.8 us (96%)
  between operations  1.39 us (2%)
  local copies, waits for them, and re-layouts  1.34 us (2%)
    pallas_call x1, Pallas kernels, train(): pl.pallas_call(train_kernel, out_shape=(block, row, block, row, table, ta...  70.7 us

profile of v3, /device:TPU:1, one launch (start us, length us, event | category | flops | bytes accessed | tf_op | source)
XLA Modules:
  0.0 74.6 jit_solution(3964374340915485087)
XLA Ops:
  0.6 0.0 copy-start.6
  0.6 0.0 copy-start.7
  0.7 0.0 copy-start.10
  0.7 0.0 copy-start.11
  0.7 0.0 copy-start.12
  0.7 0.6 copy-done.6
  1.3 0.0 copy-done.7
  1.3 0.0 copy-done.10
  1.3 0.0 copy-done.11
  1.3 0.0 copy-done.12
  1.4 0.0 copy-start.2
  1.4 0.0 copy-start.3
  1.4 0.0 copy-start.4
  1.4 0.0 copy-start.5
  1.4 70.7 %train_two_rounds.1 = (f32[400,128]{1,0:T(8,128)S(1)}, f32[1,128]{1,0:T(1,128)S(1)}, f32[400,128]{1,0:T(8,128)S(1)}, f32[1,128]{1,0:T(1,128)S(1)}, f32[400,256]{...) custom-call(f32[400,128]{1,0:T(8,128)} %bitcast.41, f32[1,128]{1,0:T(1,128)S(1)} %bitcast.57, ...), custom_call_target="tpu_custom_call" | custom-call | tf_op jit(solution)/shard_map/train_two_rounds/pallas_call | solution.py:861
  72.7 0.0 copy-start.9
  72.8 0.0 copy-start.8
  72.8 0.0 copy-done.2
  72.8 0.0 copy-done.3
  72.8 0.0 copy-done.4
  72.8 0.0 copy-done.5
  72.8 0.6 copy-done.9
  73.4 0.0 copy-done.8
  73.5 1.1 %settle.1 = (f32[400,128]{1,0:T(8,128)}, f32[1,128]{1,0:T(1,128)}, f32[400,128]{1,0:T(8,128)}, f32[1,128]{1,0:T(1,128)}, f32[400,256]{1,0:T(8,128)}, /*index=5*/f32[400,256]{1,0:T(8,128)}) custom-call(f32[400,128]{1,0:T(8,128)S(1)} %bitcast.54, f32[1,128]{1,0:T(1,128)S(1)} %get-tuple-element.107.refs_1_, f32[400,128]{1,0:T(8,128)S(1)} %bitcast.51, ...), custom_call_target="tpu_custom_call" | custom-call | tf_op jit(solution)/shard_map/settle/pallas_call | solution.py:901
  (1 shorter events, 0.0 us)
Async XLA Ops:
  0.6 0.7 copy-start.6
  0.6 0.7 copy-start.7
  0.7 0.7 copy-start.10
  0.7 0.7 copy-start.11
  0.7 0.7 copy-start.12
  1.4 71.4 %copy-start.2 = (f32[256,400]{0,1:T(8,128)S(1)}, f32[256,400]{0,1:T(8,128)}, u32[]{:S(2)}) copy-start(f32[256,400]{0,1:T(8,128)} %param.17) | copy-start | bytes 1228804
  1.4 71.4 %copy-start.3 = (f32[128,400]{0,1:T(8,128)S(1)}, f32[128,400]{0,1:T(8,128)}, u32[]{:S(2)}) copy-start(f32[128,400]{0,1:T(8,128)} %param.15) | copy-start | bytes 614404
  1.4 71.4 %copy-start.4 = (f32[256,400]{0,1:T(8,128)S(1)}, f32[256,400]{0,1:T(8,128)}, u32[]{:S(2)}) copy-start(f32[256,400]{0,1:T(8,128)} %param.18) | copy-start | bytes 1228804
  1.4 71.4 %copy-start.5 = (f32[128,400]{0,1:T(8,128)S(1)}, f32[128,400]{0,1:T(8,128)}, u32[]{:S(2)}) copy-start(f32[128,400]{0,1:T(8,128)} %param.13) | copy-start | bytes 614404
  72.7 0.7 copy-start.9
  72.8 0.7 copy-start.8

commit v4 on v3

--- a/solution.py
+++ b/solution.py
@@ -27,6 +27,11 @@
 f32, bf16, i32 = jnp.float32, jnp.bfloat16, jnp.int32
 NA, NB = 208, 192
 A, B = pl.ds(0, NA), pl.ds(NA, NB)
+PLANE = sorted(
+    ((dx, dy) for dx in range(4) for dy in range(4) if dx or dy),
+    key=lambda o: -min(o[0], 4 - o[0]) - min(o[1], 4 - o[1]),
+)
+DEPTH = (4, 3, 5, 2, 6, 1, 7)
 
 
 def remote(src, dst, send, recv, pair, edge):
@@ -456,20 +461,23 @@
         self.o, self.oup, self.ofar, self.odown = (4 + v for v in (self.y, self.up, self.far, self.down))
         self.twin = (pair + 1 - 2 * self.core, edge)
         self.plane = []
-        for d in range(1, 16):
-            c = lax.rem(self.chip + d, 16)
+        for dx, dy in PLANE:
+            c = self.chip_at(dx, dy)
             self.plane.append((self.z * 4 + (c // 8) * 2 + self.core, lax.rem(c, 8)))
-        self.depth = [(lax.rem(pair + 4 * d, GROUPS), edge) for d in range(1, 8)]
+        self.depth = [(lax.rem(pair + 4 * d, GROUPS), edge) for d in DEPTH]
         self.peers = [(pair, lax.rem(edge + d, MEMBERS)) for d in range(1, MEMBERS)]
 
     def group(self, distance):
         return (lax.rem(self.pair + distance + GROUPS, GROUPS), self.edge)
 
+    def chip_at(self, dx, dy):
+        return lax.rem(self.chip // 4 + dx, 4) * 4 + lax.rem(self.y + dy, 4)
+
     def member(self, slot):
         return (self.pair, lax.rem(slot + 4 * self.x, MEMBERS))
 
     def met(self):
-        return self.plane + self.depth + [self.twin] + [self.group(d) for d in (1, -1, 2, -2)]
+        return self.depth + self.plane + [self.twin] + [self.group(d) for d in (1, -1, 2, -2)]
 
 
 def spread(here, rows, mail):
@@ -482,6 +490,7 @@
     me = here.y
     go(0, me, A, o)
     go(1, me, B, far), go(2, me, B, up), go(3, me, B, down)
+    yield
     go(4, me, B, o)
     go(5, me, A, far), go(6, me, A, up), go(7, me, A, down)
     yield
@@ -559,13 +568,13 @@
     yield
     twin.take(0)
     mine[...] = (share[core].astype(f32) + from_twin[...].astype(f32)).astype(bf16)
-    for d, device in enumerate(here.plane):
-        first.post(d, mine.at[lax.rem(chip + d + 1, 16)], from_plane.at[chip], device)
+    for k, (dx, dy) in enumerate(PLANE):
+        first.post(k, mine.at[here.chip_at(dx, dy)], from_plane.at[chip], here.plane[k])
     yield
     total = mine[chip].astype(f32)
-    for d in range(15):
-        first.take(d)
-        total = total + from_plane[lax.rem(chip + 15 - d, 16)].astype(f32)
+    for k, (dx, dy) in reversed(list(enumerate(PLANE))):
+        first.take(k)
+        total = total + from_plane[here.chip_at(4 - dx, 4 - dy)].astype(f32)
     from_depth[z] = total.astype(bf16)
     for d, device in enumerate(here.depth):
         second.post(d, from_depth.at[z], from_depth.at[z], device)
@@ -576,10 +585,10 @@
         third.post(d, whole.at[core, chip], whole.at[core, chip], device)
     twin.post(16, whole.at[core, chip], whole.at[core, chip], here.twin)
     yield
-    for d in range(15):
-        third.take(d)
-        chunk = whole.at[core, lax.rem(chip + 15 - d, 16)]
-        twin.post(1 + d, chunk, chunk, here.twin)
+    for k, (dx, dy) in reversed(list(enumerate(PLANE))):
+        third.take(k)
+        chunk = whole.at[core, here.chip_at(4 - dx, 4 - dy)]
+        twin.post(1 + k, chunk, chunk, here.twin)
     yield
     twin.take(*range(1, 17))
     for mail in (twin, first, second, third):
@@ -716,9 +725,10 @@
 
     id_mail, id2_mail, moves = Mail(id_send, id_recv), Mail(id2_send, id2_recv), Mail(move_send, move_recv)
     ahead, behind = here.group(1), here.group(-1)
+    gather = spread(here, rows1, Mail(spread1_send, spread1_recv))
+    next(gather)
     for d, device in enumerate(here.peers):
         id_mail.post(d, ids1.at[edge], ids1.at[edge], device)
-    gather = spread(here, rows1, Mail(spread1_send, spread1_recv))
     next(gather)
     moves.post(0, ids1.at[edge], ids2.at[edge], ahead)
     fetch[9].wait()
@@ -782,6 +792,7 @@
     rows2[:, columns(here.y)] = right_two.astype(bf16)
     gather = spread(here, rows2, Mail(spread2_send, spread2_recv))
     next(gather)
+    next(gather)
     moves.take(2, 3)
     left_two[...] = in_left[...].astype(f32)
     left_two_state[...] = in_states[0, 0:1, :]
@@ -793,9 +804,11 @@
     right_parts(0, query, weight, parts2)
     folding = fold(here, parts2, total, *fold2)
     next(folding)
+    half = 4 * SHARE
+    grad = nt(rows2[:, :half], weight[:, :half])
     next(gather, None)
     weigh(1, rows2, often2, target2, query_t, weight)
-    grad = nt(rows2[...], weight[...])
+    grad = grad + nt(rows2[:, half:], weight[:, half:])
     gr, gi, sr, si = grad[:H], grad[H:], source[:H], source[H:]
     back = jnp.concatenate([gr * sr + gi * si, gi * sr - gr * si], axis=0).astype(bf16)
     last = jnp.broadcast_to(late1 + late2, (512 - D, SHARE))
@@ -808,8 +821,8 @@
         if c is not here.core:
             next(reducing)
     right_parts(1, query, weight, parts2)
+    next(reducing)
     next(folding)
-    next(reducing)
     kr, ki = operator[:H], operator[H:]
     back = jnp.concatenate([gr * kr + gi * ki, gi * kr - gr * ki], axis=0).astype(bf16)
     left_sum = nt(back, source_hot2[...])

time: 74.8 us -> 71.2 us (0.952)
  Pallas kernels: 71.8 us -> 68.2 us
    pallas_call x1, Pallas kernels: 70.7 us -> 67.1 us  [train(): pl.pallas_call(train_kernel, out_shape=(block, row, block, row, table, ta...]
where the time goes in v4:
time: 71.2 us; the launch traced here: 70.9 us
  Pallas kernels  68.2 us (96%)
  between operations  1.39 us (2%)
  local copies, waits for them, and re-layouts  1.34 us (2%)
    pallas_call x1, Pallas kernels, train(): pl.pallas_call(train_kernel, out_shape=(block, row, block, row, table, ta...  67.1 us

profile of v4, /device:TPU:1, one launch (start us, length us, event | category | flops | bytes accessed | tf_op | source)
XLA Modules:
  0.0 70.9 jit_solution(2426947397760958747)
XLA Ops:
  0.6 0.0 copy-start.6
  0.6 0.0 copy-start.7
  0.7 0.0 copy-start.10
  0.7 0.0 copy-start.11
  0.7 0.0 copy-start.12
  0.7 0.6 copy-done.6
  1.3 0.0 copy-done.7
  1.3 0.0 copy-done.10
  1.3 0.0 copy-done.11
  1.3 0.0 copy-done.12
  1.4 0.0 copy-start.2
  1.4 0.0 copy-start.3
  1.4 0.0 copy-start.4
  1.4 0.0 copy-start.5
  1.4 67.1 %train_two_rounds.1 = (f32[400,128]{1,0:T(8,128)S(1)}, f32[1,128]{1,0:T(1,128)S(1)}, f32[400,128]{1,0:T(8,128)S(1)}, f32[1,128]{1,0:T(1,128)S(1)}, f32[400,256]{...) custom-call(f32[400,128]{1,0:T(8,128)} %bitcast.41, f32[1,128]{1,0:T(1,128)S(1)} %bitcast.57, ...), custom_call_target="tpu_custom_call" | custom-call | tf_op jit(solution)/shard_map/train_two_rounds/pallas_call | solution.py:874
  69.1 0.0 copy-start.9
  69.1 0.0 copy-start.8
  69.2 0.0 copy-done.2
  69.2 0.0 copy-done.3
  69.2 0.0 copy-done.4
  69.2 0.0 copy-done.5
  69.2 0.6 copy-done.9
  69.8 0.0 copy-done.8
  69.8 1.1 %settle.1 = (f32[400,128]{1,0:T(8,128)}, f32[1,128]{1,0:T(1,128)}, f32[400,128]{1,0:T(8,128)}, f32[1,128]{1,0:T(1,128)}, f32[400,256]{1,0:T(8,128)}, /*index=5*/f32[400,256]{1,0:T(8,128)}) custom-call(f32[400,128]{1,0:T(8,128)S(1)} %bitcast.54, f32[1,128]{1,0:T(1,128)S(1)} %get-tuple-element.107.refs_1_, f32[400,128]{1,0:T(8,128)S(1)} %bitcast.51, ...), custom_call_target="tpu_custom_call" | custom-call | tf_op jit(solution)/shard_map/settle/pallas_call | solution.py:914
  (1 shorter events, 0.0 us)
Async XLA Ops:
  0.6 0.7 copy-start.6
  0.6 0.7 copy-start.7
  0.7 0.7 copy-start.10
  0.7 0.7 copy-start.11
  0.7 0.7 copy-start.12
  1.4 67.8 %copy-start.2 = (f32[256,400]{0,1:T(8,128)S(1)}, f32[256,400]{0,1:T(8,128)}, u32[]{:S(2)}) copy-start(f32[256,400]{0,1:T(8,128)} %param.17) | copy-start | bytes 1228804
  1.4 67.8 %copy-start.3 = (f32[128,400]{0,1:T(8,128)S(1)}, f32[128,400]{0,1:T(8,128)}, u32[]{:S(2)}) copy-start(f32[128,400]{0,1:T(8,128)} %param.15) | copy-start | bytes 614404
  1.4 67.8 %copy-start.4 = (f32[256,400]{0,1:T(8,128)S(1)}, f32[256,400]{0,1:T(8,128)}, u32[]{:S(2)}) copy-start(f32[256,400]{0,1:T(8,128)} %param.18) | copy-start | bytes 1228804
  1.4 67.8 %copy-start.5 = (f32[128,400]{0,1:T(8,128)S(1)}, f32[128,400]{0,1:T(8,128)}, u32[]{:S(2)}) copy-start(f32[128,400]{0,1:T(8,128)} %param.13) | copy-start | bytes 614404
  69.1 0.7 copy-start.9
  69.1 0.7 copy-start.8

commit v5 on v4

--- a/solution.py
+++ b/solution.py
@@ -829,10 +829,10 @@
     block, state = update(left_two[...], left_two_state[...], left_sum)
     out_rows[0] = block.astype(bf16)
     out_states[1] = jnp.broadcast_to(state, (8, SHARE))
+    next(folding)
+    next(reducing)
     moves.post(4, out_rows.at[0], in_rows.at[0], behind)
     moves.post(5, out_states.at[1], in_states.at[1], behind)
-    next(folding)
-    next(reducing)
     next(folding)
     next(reducing)
     next(folding, None)

time: 71.2 us -> 71.2 us (level)
  no operation moved by 1% of the time
where the time goes in v5:
time: 71.2 us; the launch traced here: 70.9 us
  Pallas kernels  68.2 us (96%)
  between operations  1.39 us (2%)
  local copies, waits for them, and re-layouts  1.34 us (2%)
    pallas_call x1, Pallas kernels, train(): pl.pallas_call(train_kernel, out_shape=(block, row, block, row, table, ta...  67.1 us

profile of v5, /device:TPU:1, one launch (start us, length us, event | category | flops | bytes accessed | tf_op | source)
XLA Modules:
  0.0 70.9 jit_solution(13190736399018243914)
XLA Ops:
  0.6 0.0 copy-start.6
  0.6 0.0 copy-start.7
  0.7 0.0 copy-start.10
  0.7 0.0 copy-start.11
  0.7 0.0 copy-start.12
  0.7 0.6 copy-done.6
  1.3 0.0 copy-done.7
  1.3 0.0 copy-done.10
  1.3 0.0 copy-done.11
  1.3 0.0 copy-done.12
  1.4 0.0 copy-start.2
  1.4 0.0 copy-start.3
  1.4 0.0 copy-start.4
  1.4 0.0 copy-start.5
  1.4 67.1 %train_two_rounds.1 = (f32[400,128]{1,0:T(8,128)S(1)}, f32[1,128]{1,0:T(1,128)S(1)}, f32[400,128]{1,0:T(8,128)S(1)}, f32[1,128]{1,0:T(1,128)S(1)}, f32[400,256]{...) custom-call(f32[400,128]{1,0:T(8,128)} %bitcast.41, f32[1,128]{1,0:T(1,128)S(1)} %bitcast.57, ...), custom_call_target="tpu_custom_call" | custom-call | tf_op jit(solution)/shard_map/train_two_rounds/pallas_call | solution.py:874
  69.1 0.0 copy-start.9
  69.1 0.0 copy-start.8
  69.2 0.0 copy-done.2
  69.2 0.0 copy-done.3
  69.2 0.0 copy-done.4
  69.2 0.0 copy-done.5
  69.2 0.6 copy-done.9
  69.8 0.0 copy-done.8
  69.8 1.1 %settle.1 = (f32[400,128]{1,0:T(8,128)}, f32[1,128]{1,0:T(1,128)}, f32[400,128]{1,0:T(8,128)}, f32[1,128]{1,0:T(1,128)}, f32[400,256]{1,0:T(8,128)}, /*index=5*/f32[400,256]{1,0:T(8,128)}) custom-call(f32[400,128]{1,0:T(8,128)S(1)} %bitcast.54, f32[1,128]{1,0:T(1,128)S(1)} %get-tuple-element.107.refs_1_, f32[400,128]{1,0:T(8,128)S(1)} %bitcast.51, ...), custom_call_target="tpu_custom_call" | custom-call | tf_op jit(solution)/shard_map/settle/pallas_call | solution.py:914
  (1 shorter events, 0.0 us)
Async XLA Ops:
  0.6 0.7 copy-start.6
  0.6 0.7 copy-start.7
  0.7 0.7 copy-start.10
  0.7 0.7 copy-start.11
  0.7 0.7 copy-start.12
  1.4 67.8 %copy-start.2 = (f32[256,400]{0,1:T(8,128)S(1)}, f32[256,400]{0,1:T(8,128)}, u32[]{:S(2)}) copy-start(f32[256,400]{0,1:T(8,128)} %param.17) | copy-start | bytes 1228804
  1.4 67.8 %copy-start.3 = (f32[128,400]{0,1:T(8,128)S(1)}, f32[128,400]{0,1:T(8,128)}, u32[]{:S(2)}) copy-start(f32[128,400]{0,1:T(8,128)} %param.15) | copy-start | bytes 614404
  1.4 67.8 %copy-start.4 = (f32[256,400]{0,1:T(8,128)S(1)}, f32[256,400]{0,1:T(8,128)}, u32[]{:S(2)}) copy-start(f32[256,400]{0,1:T(8,128)} %param.18) | copy-start | bytes 1228804
  1.4 67.8 %copy-start.5 = (f32[128,400]{0,1:T(8,128)S(1)}, f32[128,400]{0,1:T(8,128)}, u32[]{:S(2)}) copy-start(f32[128,400]{0,1:T(8,128)} %param.13) | copy-start | bytes 614404
  69.1 0.7 copy-start.9
  69.1 0.7 copy-start.8
